TPU v7x, 128 devices: a whole 4x4x4 slice. The times are simulated.
128 devices in a mesh: row: 16 (over z, y), col: 8 (over x, core).
Axes of the slice: x: 4, y: 4, z: 4, core: 2. Of those that a mesh axis runs over, the one named last changes fastest.
Arguments:
- rhs: float32 [131072, 256], P(('row', 'col')), may hold values from -8 to 8
- front_factor: float32 [131072, 1024], P(('row', 'col')), may hold values from -1 to 4, as said below
- coupling: bfloat16 [229376, 1024], P(('row', 'col')), may hold values from -0.1875 to 0.1875
- bound_count: int32 [128], P(('row', 'col')), may hold values from 448 to 1792, as said below
- sep_owner: int32 [128, 64], P(('row', 'col')), may hold values from 0 to 127, as said below
- sep_index: int32 [128, 1792], P(('row', 'col')), may hold values from 0 to 511
- sep_rhs: float32 [65536, 256], P(('row', 'col')), may hold values from -6 to 6
- sep_factor: float32 [65536, 512], P(('row', 'col')), may hold values from -1 to 4, as said below
- cell_weight: float32 [16384, 8], P(('row', 'col')), may hold values from 0.02 to 0.3
- cell_pivot: int32 [16384, 8], P(('row', 'col')), may hold values from 0 to 1023
Outputs:
- sep_potential: float32 [65536, 256], P(('row', 'col'))
- hess: float32 [16384, 16384], P('row', 'col')
Inputs may be any that keep to these rules, and one draw needn't show every extreme that they name: `front_factor`: each block of 1024 rows is lower triangular with diagonal entries 1 or more. `sep_factor`: each block of 512 rows is lower triangular with diagonal entries 1 or more. `bound_count`: some front has all 1792 boundary rows live. `sep_owner`: each row names 64 distinct separator blocks.
All inputs are finite; a program needn't handle non-finite values.
Results may differ from a plain program's by a relative error of at most 0.0031.
Values may be sent and summed in bfloat16 or wider, within the bound.
No kernel may reach another device: no remote copies, remote signals or barrier semaphores. Data moves between devices by JAX's collectives and lax.ppermute only.
A program may use at most 128 MiB of HBM per device.

v0:
```python
import jax
import jax.numpy as jnp
from jax import lax
from jax.sharding import PartitionSpec as P


def front_solve(factor, right):
    half_way = jax.scipy.linalg.solve_triangular(factor, right, lower=True)
    return jax.scipy.linalg.solve_triangular(factor, half_way, trans=1, lower=True)


def local(
    rhs,
    front_factor,
    coupling,
    bound_count,
    sep_owner,
    sep_index,
    sep_rhs,
    sep_factor,
    cell_weight,
    cell_pivot,
):
    row_count = lax.axis_size("row")
    col_count = lax.axis_size("col")
    fronts = row_count * col_count
    bound = coupling.shape[0]
    sources = rhs.shape[1]
    sep_size = sep_rhs.shape[0]
    halves = sep_owner.shape[1]
    slots = bound // halves
    living = jnp.arange(bound, dtype=jnp.int32) < bound_count[0]
    live_float = living.astype(jnp.float32)[:, None]
    live_half = living.astype(jnp.bfloat16)[:, None]
    owners = sep_owner[0]
    solved = front_solve(front_factor, rhs).astype(jnp.bfloat16)
    contrib = (jnp.dot(coupling, solved, preferred_element_type=jnp.float32) * live_float).astype(
        jnp.bfloat16
    )
    outgoing = (
        jnp.zeros((fronts, slots, sources), jnp.bfloat16)
        .at[owners]
        .set(contrib.reshape(halves, slots, sources))
    )
    out_index = (
        jnp.zeros((fronts, slots), jnp.int32).at[owners].set(sep_index[0].reshape(halves, slots))
    )
    incoming, in_index = (
        lax.all_to_all(outgoing, ("row", "col"), split_axis=0, concat_axis=0, tiled=True),
        lax.all_to_all(out_index, ("row", "col"), split_axis=0, concat_axis=0, tiled=True),
    )
    received = incoming.reshape(fronts * slots, sources)
    flat_index = in_index.reshape(fronts * slots)
    selector = (jnp.arange(sep_size, dtype=jnp.int32)[:, None] == flat_index[None, :]).astype(
        jnp.bfloat16
    )
    totals = jnp.dot(selector, received, preferred_element_type=jnp.float32)
    sep_potential = front_solve(sep_factor, sep_rhs - totals)
    sep_half = sep_potential.astype(jnp.bfloat16)
    replies = lax.dot_general(
        selector, sep_half, (((0,), (0,)), ((), ())), preferred_element_type=jnp.float32
    ).astype(jnp.bfloat16)
    returned = lax.all_to_all(
        replies.reshape(fronts, slots, sources),
        ("row", "col"),
        split_axis=0,
        concat_axis=0,
        tiled=True,
    )
    values = returned[owners].reshape(bound, sources) * live_half
    lifted = lax.dot_general(
        coupling, values, (((0,), (0,)), ((), ())), preferred_element_type=jnp.float32
    )
    potential = front_solve(front_factor, rhs - lifted)
    picked = potential[cell_pivot]
    field = jnp.sum(cell_weight[:, :, None] * picked, axis=1).astype(jnp.bfloat16)
    scale = 1.0 / sources
    cell_rows = field.shape[0]
    every = lax.all_gather(field, ("row", "col"), axis=0, tiled=True)
    layered = every.reshape(row_count, col_count, cell_rows, sources)
    row_tile = lax.dynamic_index_in_dim(layered, lax.axis_index("row"), 0, keepdims=False).reshape(
        col_count * cell_rows, sources
    )
    col_tile = lax.dynamic_index_in_dim(layered, lax.axis_index("col"), 1, keepdims=False).reshape(
        row_count * cell_rows, sources
    )
    gram = (
        lax.dot_general(
            row_tile, col_tile, (((1,), (1,)), ((), ())), preferred_element_type=jnp.float32
        )
        * scale
    )
    hess = gram * gram
    return (sep_potential, hess)


def solution(mesh):
    placed = (
        P(("row", "col"), None),
        P(("row", "col"), None),
        P(("row", "col"), None),
        P(("row", "col")),
        P(("row", "col"), None),
        P(("row", "col"), None),
        P(("row", "col"), None),
        P(("row", "col"), None),
        P(("row", "col"), None),
        P(("row", "col"), None),
    )
    return jax.shard_map(
        local,
        mesh=mesh,
        in_specs=placed,
        out_specs=(P(("row", "col"), None), P("row", "col")),
        check_vma=False,
    )
```

profile of v0, /device:TPU:0, one launch (start us, length us, event | category | flops | bytes accessed | tf_op | source)
XLA Modules:
  0.0 382.8 jit_solution(9803424491787605335)
XLA Ops:
  10.0 11.1 %all-to-all-start = ((s32[128,1,28]{2,1,0:T(1,128)}), s32[128,1,28]{2,1,0:T(1,128)S(1)}, u32[]{:S(2)}, u32[]{:S(2)}) async-start(s32[128,1,28]{2,1,0:T(1,128)} %bitcast.3), calls=%async_computation | async-start | bytes 131072 | tf_op jit(solution)/shard_map/all_to_all | solution.py:50
  21.1 4.9 %fusion.3 = f32[1024,1024]{1,0:T(8,128)} fusion(f32[1024,1024]{1,0:T(8,128)} %param.15), kind=kLoop, calls=%fused_computation.14 | loop fusion | flops 2097152 | bytes 8388608 | tf_op jit(solution)/shard_map/jit(_solve_triangular)/triangular_solve | solution.py:9
  26.0 24.0 %while.10 = (s32[]{:T(128)}, f32[1024,1024]{1,0:T(8,128)}, s32[8,2]{0,1:T(2,128)S(1)}, f32[8,128,128]{2,1,0:T(8,128)S(1)}, s32[]{:T(128)}) while((s32[]{:T(128)}, f32[1024,1024]{1,0:T(8,128)}, s32[8,2]{0,1:T(2,128)S(1)}, f32[8,128,128]{2,1,0:T(8,128)S(1)}, s32[]{:T(128)}) %tuple.93), condition=%wide.while_cond.1, body=%wide.while_body.1.sunk | while | flops 2 | bytes 131181 | solution.py:9
  26.7 2.3 bitcast_dynamic-update-slice_fusion.5
  29.7 2.3 bitcast_dynamic-update-slice_fusion.5
  32.7 2.3 bitcast_dynamic-update-slice_fusion.5
  35.7 2.3 bitcast_dynamic-update-slice_fusion.5
  38.7 2.3 bitcast_dynamic-update-slice_fusion.5
  41.8 2.3 bitcast_dynamic-update-slice_fusion.5
  44.8 2.3 bitcast_dynamic-update-slice_fusion.5
  47.8 2.3 bitcast_dynamic-update-slice_fusion.5
  50.1 79.1 %custom-call.17 = f32[8,128,128]{1,2,0:T(8,128)S(1)} custom-call(f32[8,128,128]{2,1,0:T(8,128)S(1)} %get-tuple-element.41), custom_call_target="InvertDiagBlocksLowerTriangular" | custom-call | tf_op jit(solution)/shard_map/jit(_solve_triangular)/triangular_solve | solution.py:9
  148.9 8.3 %scatter_fusion = bf16[128,28,256]{2,1,0:T(8,128)(2,1)} fusion(bf16[128,28,256]{2,1,0:T(8,128)(2,1)} %broadcast_in_dim.7, s32[64]{0:T(128)S(1)} %fusion.171, bf16[64,28,256]{2,1,0:T(8,128)(2,1)S(1)} %reshape.222), kind=kCustom, calls=%fused_computation.3 | custom fusion | bytes 2752768 | tf_op jit(solution)/shard_map/scatter | solution.py:43
  157.2 9.7 %all-to-all-start.1 = ((bf16[128,28,256]{2,1,0:T(8,128)(2,1)}), bf16[128,28,256]{2,1,0:T(8,128)(2,1)S(1)}, u32[]{:S(2)}, u32[]{:S(2)}) async-start(bf16[128,28,256]{2,1,0:T(8,128)(2,1)} %scatter_fusion), calls=%async_computation.1 | async-start | bytes 4194304 | tf_op jit(solution)/shard_map/all_to_all | solution.py:49
  167.0 2.3 fusion.11
  169.3 11.7 %while.9 = (s32[]{:T(128)}, f32[512,512]{1,0:T(8,128)}, s32[4,2]{0,1:T(2,128)S(1)}, f32[4,128,128]{2,1,0:T(8,128)S(1)}, s32[]{:T(128)}) while((s32[]{:T(128)}, f32[512,512]{1,0:T(8,128)}, s32[4,2]{0,1:T(2,128)S(1)}, f32[4,128,128]{2,1,0:T(8,128)S(1)}, s32[]{:T(128)}) %tuple.96), condition=%wide.while_cond.2, body=%wide.while_body.2.sunk | while | flops 2 | bytes 131181 | solution.py:9
  170.0 2.3 bitcast_dynamic-update-slice_fusion.4
  172.9 2.3 bitcast_dynamic-update-slice_fusion.4
  175.9 2.3 bitcast_dynamic-update-slice_fusion.4
  178.8 2.2 bitcast_dynamic-update-slice_fusion.4
  181.0 39.3 %custom-call.13 = f32[4,128,128]{1,2,0:T(8,128)S(1)} custom-call(f32[4,128,128]{2,1,0:T(8,128)S(1)} %get-tuple-element.27), custom_call_target="InvertDiagBlocksLowerTriangular" | custom-call | tf_op jit(solution)/shard_map/jit(_solve_triangular)/triangular_solve | solution.py:9
  223.3 2.9 fusion.9
  230.8 2.1 fusion.2
  234.4 9.8 %all-to-all-start.2 = ((bf16[128,28,256]{2,1,0:T(8,128)(2,1)}), bf16[128,28,256]{2,1,0:T(8,128)(2,1)S(1)}, u32[]{:S(2)}, u32[]{:S(2)}) async-start(bf16[128,28,256]{2,1,0:T(8,128)(2,1)} %reshape.126), calls=%async_computation.2 | async-start | bytes 4194304 | tf_op jit(solution)/shard_map/all_to_all | solution.py:63
  244.3 2.6 copy.20
  247.2 27.4 %all-to-all-done.2 = bf16[128,28,256]{2,1,0:T(8,128)(2,1)S(1)} async-done(((bf16[128,28,256]{2,1,0:T(8,128)(2,1)}), bf16[128,28,256]{2,1,0:T(8,128)(2,1)S(1)}, u32[]{:S(2)}, u32[]{:S(2)}) %all-to-all-start.2) | async-done | bytes 1835040 | tf_op jit(solution)/shard_map/all_to_all | solution.py:63
  274.6 1.6 gather_fusion
  277.7 3.7 fusion.8
  289.2 1.7 convolution_subtract_fusion.31
  298.6 3.5 gather_fusion.1
  303.1 65.6 %all-gather.2.cloned.1.call-done = bf16[16384,256]{1,0:T(8,128)(2,1)} async-done(((bf16[128,256]{1,0:T(8,128)(2,1)}), bf16[16384,256]{1,0:T(8,128)(2,1)}) %all-gather.2.cloned.1.call-update) | async-done | bytes 8388624 | tf_op jit(solution)/shard_map/all_gather | solution.py:79
  371.0 4.7 %multiply_multiply_fusion = f32[1024,2048]{1,0:T(8,128)} fusion(bf16[1024,256]{1,0:T(8,128)(2,1)S(1)} %bitcast.240, bf16[2048,256]{1,0:T(8,128)(2,1)S(1)} %bitcast.239), kind=kOutput, calls=%fused_computation.8 | convolution fusion | flops 1077936128 | bytes 9961472 | tf_op jit(solution)/shard_map/dot_general | solution.py:88
  (193 shorter events, 58.7 us)
Async XLA Ops:
  10.0 147.2 %all-to-all-start = ((s32[128,1,28]{2,1,0:T(1,128)}), s32[128,1,28]{2,1,0:T(1,128)S(1)}, u32[]{:S(2)}, u32[]{:S(2)}) async-start(s32[128,1,28]{2,1,0:T(1,128)} %bitcast.3), calls=%async_computation | async-start | bytes 131072 | tf_op jit(solution)/shard_map/all_to_all | solution.py:50
  21.1 108.0 %copy-start.3 = (f32[1024,256]{1,0:T(8,128)S(1)}, f32[1024,256]{1,0:T(8,128)}, u32[]{:S(2)}) copy-start(f32[1024,256]{1,0:T(8,128)} %param.14) | copy-start | bytes 3145732
  129.2 5.1 %copy-start = (f32[1024,1024]{1,0:T(8,128)S(1)}, f32[1024,1024]{1,0:T(8,128)}, u32[]{:S(2)}) copy-start(f32[1024,1024]{1,0:T(8,128)} %get-tuple-element.217) | copy-start | bytes 12582916
  141.9 3.4 copy-start.7
  157.2 64.6 %all-to-all-start.1 = ((bf16[128,28,256]{2,1,0:T(8,128)(2,1)}), bf16[128,28,256]{2,1,0:T(8,128)(2,1)S(1)}, u32[]{:S(2)}, u32[]{:S(2)}) async-start(bf16[128,28,256]{2,1,0:T(8,128)(2,1)} %scatter_fusion), calls=%async_computation.1 | async-start | bytes 4194304 | tf_op jit(solution)/shard_map/all_to_all | solution.py:49
  223.3 3.2 copy-start.2
  230.8 3.7 copy-start.4
  232.9 13.9 %copy-start.6 = (s32[128,8]{0,1:T(8,128)S(1)}, s32[128,8]{0,1:T(8,128)}, u32[]{:S(2)}) copy-start(s32[128,8]{0,1:T(8,128)} %param.23) | copy-start | bytes 12292
  234.4 12.6 %copy-start.5 = (f32[128,8]{0,1:T(8,128)S(1)}, f32[128,8]{0,1:T(8,128)}, u32[]{:S(2)}) copy-start(f32[128,8]{0,1:T(8,128)} %param.22) | copy-start | bytes 12292
  234.4 40.1 %all-to-all-start.2 = ((bf16[128,28,256]{2,1,0:T(8,128)(2,1)}), bf16[128,28,256]{2,1,0:T(8,128)(2,1)S(1)}, u32[]{:S(2)}, u32[]{:S(2)}) async-start(bf16[128,28,256]{2,1,0:T(8,128)(2,1)} %reshape.126), calls=%async_computation.2 | async-start | bytes 4194304 | tf_op jit(solution)/shard_map/all_to_all | solution.py:63
  244.2 124.4 %all-gather.2.cloned.1.call-start = ((), (), s32[]{:S(2)}) async-start(), calls=%async_computation.3 | async-start | bytes 8454144 | tf_op jit(solution)/shard_map/all_gather | solution.py:79
  277.7 4.1 %copy-start.1 = (f32[1024,1024]{1,0:T(8,128)S(1)}, f32[1024,1024]{1,0:T(8,128)}, u32[]{:S(2)}) copy-start(f32[1024,1024]{1,0:T(8,128)} %get-tuple-element.217) | copy-start | bytes 12582916
Sparse Core Ops, SparseCore 0:
  303.2 65.3 all-gather.1
where the time goes:
time: 389 us; the launch traced here: 383 us
  other arithmetic  129 us (33%)
  waiting for transfers between devices  93 us (24%)
  local copies, waits for them, and re-layouts  63.8 us (16%)
  matrix products  50 us (13%)
  starting transfers between devices  30.7 us (8%)
  between operations  16.2 us (4%)
    another operation x8, other arithmetic, front_solve(): jax.scipy.linalg.solve_triangular(factor, half_way, trans=1, lower=True)  126 us
    all_gather x1, waiting for transfers between devices, local(): every = lax.all_gather(field, ('row', 'col'), axis=0, tiled=True)  65.6 us
    all_to_all x1, waiting for transfers between devices, local(): lax.all_to_all(replies.reshape(fronts, slots, sources), ('row', 'col'), s...  27.4 us
    another operation x34, local copies, waits for them, and re-layouts, front_solve(): jax.scipy.linalg.solve_triangular(factor, half_way, trans=1, lower=True)  24.2 us
    another operation x37, matrix products, front_solve(): half_way = jax.scipy.linalg.solve_triangular(factor, right, lower=True)  20.1 us
    another operation x37, matrix products, front_solve(): jax.scipy.linalg.solve_triangular(factor, half_way, trans=1, lower=True)  15.3 us
    another operation x12, local copies, waits for them, and re-layouts  11.6 us
    all_to_all x1, starting transfers between devices, local(): lax.all_to_all(out_index, ('row', 'col'), split_axis=0, concat_axis=0, ti...  11.1 us
  transfers between devices with their start and end apart: 4, of which 2 were waited for; matrix products, arithmetic and copies ran while one was open for 50% of the time, Pallas kernels for 0%

commit v1 on v0

v1 whole, which is shorter than its diff:
```python
import jax
import jax.numpy as jnp
from jax import lax
from jax.experimental import pallas as pl
from jax.experimental.pallas import tpu as pltpu
from jax.sharding import PartitionSpec as P

F32 = jnp.float32
BF16 = jnp.bfloat16
NN = (((1,), (0,)), ((), ()))
NT = (((1,), (1,)), ((), ()))
BASE = 256
PAD = 32
LANES = 128
VMEM = pltpu.VMEM
SMEM = pltpu.SMEM


def mm(a, b, dims=NN):
    return lax.dot_general(a, b, dims, preferred_element_type=F32)


def split(x):
    high = x.astype(BF16)
    return high, (x - high.astype(F32)).astype(BF16)


def mm3(a, b, dims=NN):
    return mm(a[0], b[0], dims) + (mm(a[0], b[1], dims) + mm(a[1], b[0], dims))


def invert_lower(blocks):
    order = blocks[0].shape[0]
    row = lax.broadcasted_iota(jnp.int32, (order, order), 0)
    col = lax.broadcasted_iota(jnp.int32, (order, order), 1)

    def below(level):
        same = (row >> (level + 1)) == (col >> (level + 1))
        return same & (((row >> level) & 1) == 1) & (((col >> level) & 1) == 0)

    found = []
    mask = below(0)
    for block in blocks:
        diagonal = jnp.where(row == col, block, 0.0)
        down = 1.0 / jnp.sum(diagonal, axis=1, keepdims=True)
        across = 1.0 / jnp.sum(diagonal, axis=0, keepdims=True)
        pairs = jnp.where(mask, -(down * block * across), 0.0)
        found.append(jnp.where(row == col, down, pairs))
    level = 1
    while (1 << level) < order:
        mask = below(level)
        parts = [split(one) for one in found]
        halves = [
            mm3(part, split(jnp.where(mask, block, 0.0))) for part, block in zip(parts, blocks)
        ]
        found = [one - mm3(split(half), part) for one, half, part in zip(found, halves, parts)]
        level += 1
    return found


def place_rows(source, target, owner_ref, count, slots, halves):
    width = source.shape[1]
    row = lax.broadcasted_iota(jnp.int32, (PAD, width), 0)
    for j in range(halves):
        rows = source[slots * j : slots * j + PAD, :]
        keep = (row < slots) & (row < count - slots * j)
        target[owner_ref[0, j]] = jnp.where(keep, rows, 0.0).astype(target.dtype)


def forward_kernel(
    owner_ref, count_ref, factor, rhs, coupling, out, high_out, low_out,
    diag, lower, right, block, high, low, contrib, sems,
):
    half = diag.shape[1]
    bound = coupling.shape[0]
    halves = owner_ref.shape[1]
    copies = [
        pltpu.make_async_copy(factor.at[0:half, 0:half], diag.at[0], sems.at[0]),
        pltpu.make_async_copy(factor.at[half : 2 * half, half : 2 * half], diag.at[1], sems.at[1]),
        pltpu.make_async_copy(rhs, right, sems.at[2]),
        pltpu.make_async_copy(factor.at[half : 2 * half, 0:half], lower, sems.at[3]),
        pltpu.make_async_copy(coupling, block, sems.at[4]),
    ]
    for copy in copies:
        copy.start()
    out[...] = jnp.zeros_like(out)
    contrib[bound:, :] = jnp.zeros((contrib.shape[0] - bound, contrib.shape[1]), F32)
    copies[0].wait()
    copies[1].wait()
    quarters = [
        diag[i, k * BASE : (k + 1) * BASE, k * BASE : (k + 1) * BASE]
        for i in range(2)
        for k in range(half // BASE)
    ]
    inverses = invert_lower(quarters)
    for i in range(2):
        first, second = inverses[2 * i], inverses[2 * i + 1]
        first_parts, second_parts = split(first), split(second)
        between = split(diag[i, BASE:, :BASE])
        corner = split(-mm3(second_parts, split(mm3(between, first_parts))))
        for k, ref in enumerate((high, low)):
            ref[i, :BASE, :BASE] = first_parts[k]
            ref[i, BASE:, BASE:] = second_parts[k]
            ref[i, BASE:, :BASE] = corner[k]
            ref[i, :BASE, BASE:] = jnp.zeros((BASE, BASE), BF16)
    keep = [
        pltpu.make_async_copy(high, high_out, sems.at[5]),
        pltpu.make_async_copy(low, low_out, sems.at[6]),
    ]
    for copy in keep:
        copy.start()
    copies[2].wait()
    copies[3].wait()
    inv = [(high[i], low[i]) for i in range(2)]
    off = split(lower[...])
    turned = right[...].T
    x0 = mm3(split(turned[:, :half]), inv[0], NT)
    x1 = mm3(split(turned[:, half:] - mm3(split(x0), off, NT)), inv[1], NT)
    y1 = mm3(split(x1), inv[1])
    y0 = mm3(split(x0 - mm3(split(y1), off)), inv[0])
    copies[4].wait()
    contrib[:bound, :] = mm(block[:, :half], y0.astype(BF16), NT) + mm(
        block[:, half:], y1.astype(BF16), NT
    )
    place_rows(contrib, out, owner_ref, count_ref[0], bound // halves, halves)
    for copy in keep:
        copy.wait()


def prepare_kernel(
    owner_ref, count_ref, factor, rhs, coupling, high, low, weight, pivot, sep,
    field0, g_high, g_low, s_high, s_low,
    lower, block, rows, placed, sems,
):
    half = lower.shape[0]
    bound = coupling.shape[0]
    halves = owner_ref.shape[1]
    cells = weight.shape[0]
    copies = [
        pltpu.make_async_copy(factor.at[half : 2 * half, 0:half], lower, sems.at[0]),
        pltpu.make_async_copy(coupling, block, sems.at[1]),
    ]
    for copy in copies:
        copy.start()
    first, second = invert_lower([sep[:BASE, :BASE], sep[BASE:, BASE:]])
    first_parts, second_parts = split(first), split(second)
    corner = -mm3(second_parts, split(mm3(split(sep[BASE:, :BASE]), first_parts)))
    corner_parts = split(corner)
    first_t, second_t, corner_t = split(first.T), split(second.T), split(corner.T)
    pieces = (
        (0, 0, mm3(first_t, first_parts) + mm3(corner_t, corner_parts)),
        (0, 1, mm3(corner_t, second_parts)),
        (1, 0, mm3(second_t, corner_parts)),
        (1, 1, mm3(second_t, second_parts)),
    )
    for i, k, piece in pieces:
        at = (slice(i * BASE, (i + 1) * BASE), slice(k * BASE, (k + 1) * BASE))
        s_high[at], s_low[at] = split(piece)

    places = lax.broadcasted_iota(jnp.int32, (cells, 2 * half), 1)
    project = jnp.zeros((cells, 2 * half), F32)
    for k in range(weight.shape[1]):
        project += jnp.where(places == pivot[:, k : k + 1], weight[:, k : k + 1], 0.0)
    copies[0].wait()
    inv = [(high[i], low[i]) for i in range(2)]
    off = split(lower[...])
    x0 = mm3(split(project[:, :half]), inv[0], NT)
    x1 = mm3(split(project[:, half:] - mm3(split(x0), off, NT)), inv[1], NT)
    y1 = mm3(split(x1), inv[1])
    y0 = mm3(split(x0 - mm3(split(y1), off)), inv[0])
    y0, y1 = split(y0), split(y1)
    field0[...] = mm3(y0, split(rhs[:half, :])) + mm3(y1, split(rhs[half:, :]))
    copies[1].wait()
    both = mm(block[:, :half], jnp.concatenate(y0, axis=0), NT) + mm(
        block[:, half:], jnp.concatenate(y1, axis=0), NT
    )
    rows[:bound, :] = both[:, :cells] + both[:, cells:]
    rows[bound:, :] = jnp.zeros((rows.shape[0] - bound, cells), F32)
    placed[...] = jnp.zeros_like(placed)
    place_rows(rows, placed, owner_ref, count_ref[0], bound // halves, halves)
    group = LANES // PAD
    for t in range(placed.shape[0] // group):
        tile = placed[t * group : (t + 1) * group].reshape(LANES, cells).T
        g_high[:, t * LANES : (t + 1) * LANES], g_low[:, t * LANES : (t + 1) * LANES] = split(tile)


def select_kernel(me_ref, index, sel, sel_t, *, bound, halves):
    fronts = index.shape[0]
    slots = bound // halves
    group = LANES // PAD
    me = me_ref[0]
    order = sel.shape[0]

    def one_hot(cond):
        return jnp.where(cond, 1.0, 0.0).astype(BF16)

    def owner_of(at):
        return (at * 2341) >> 16

    match = one_hot(index[:, bound : bound + halves] == me)
    spread = one_hot(
        owner_of(lax.broadcasted_iota(jnp.int32, (halves, bound), 1))
        == lax.broadcasted_iota(jnp.int32, (halves, bound), 0)
    )
    chosen = mm(match, spread)
    values = index[:, :bound]
    low = (chosen * (values & 255).astype(F32)).astype(BF16)
    high = (chosen * ((values >> 8) + 1).astype(F32)).astype(BF16)
    at = lax.broadcasted_iota(jnp.int32, (bound, LANES), 0)
    lane = lax.broadcasted_iota(jnp.int32, (bound, LANES), 1)
    fold = one_hot((at - slots * owner_of(at)) == (lane & (PAD - 1)))
    front = lax.broadcasted_iota(jnp.int32, (fronts, LANES), 0)
    part = lax.broadcasted_iota(jnp.int32, (fronts, LANES), 1) >> 5
    mine = (front & (group - 1)) == part
    low = jnp.where(mine, mm(low, fold), 0.0).astype(BF16)
    high = jnp.where(mine, mm(high, fold), 0.0).astype(BF16)
    groups = fronts // group
    gather = one_hot(
        (lax.broadcasted_iota(jnp.int32, (LANES, fronts), 1) >> 2)
        == lax.broadcasted_iota(jnp.int32, (LANES, fronts), 0)
    )
    flat = mm(gather, low) + 256.0 * (mm(gather, high) - 1.0)
    flat_t = flat.T
    flat = flat.astype(jnp.int32)
    flat_t = flat_t.astype(jnp.int32)
    down = lax.broadcasted_iota(jnp.int32, (order, LANES), 0)
    across = lax.broadcasted_iota(jnp.int32, (LANES, order), 1)
    for g in range(groups):
        sel[:, g * LANES : (g + 1) * LANES] = one_hot(down == flat[g : g + 1, :])
        sel_t[g * LANES : (g + 1) * LANES, :] = one_hot(across == flat_t[:, g : g + 1])


def separator_kernel(sel, incoming, sep_rhs, s_high, s_low, sel_t, potential, replies):
    reduced = sep_rhs[...] - mm(sel[...], incoming[...])
    found = mm3((s_high[...], s_low[...]), split(reduced))
    potential[...] = found
    replies[...] = mm(sel_t[...], found.astype(BF16)).astype(BF16)


def field_kernel(field0, g_high, g_low, returned, field):
    values = returned[...]
    field[...] = (field0[...] - (mm(g_high[...], values) + mm(g_low[...], values))).astype(BF16)


def call(kernel, outs, ins, scratch, specs, out_specs, flops, moved, vmem):
    return pl.pallas_call(
        kernel,
        out_shape=outs,
        in_specs=specs,
        out_specs=out_specs,
        scratch_shapes=scratch,
        compiler_params=pltpu.CompilerParams(vmem_limit_bytes=vmem * 1024 * 1024),
        cost_estimate=pl.CostEstimate(flops=flops, bytes_accessed=moved, transcendentals=0),
    )(*ins)


def local(
    rhs, front_factor, coupling, bound_count, sep_owner, sep_index, sep_rhs, sep_factor,
    cell_weight, cell_pivot,
):
    row_count = lax.axis_size("row")
    col_count = lax.axis_size("col")
    fronts = row_count * col_count
    bound, order = coupling.shape
    sources = rhs.shape[1]
    sep_size = sep_rhs.shape[0]
    halves = sep_owner.shape[1]
    cells = cell_weight.shape[0]
    half = order // 2
    flat = fronts * PAD
    vm = pl.BlockSpec(memory_space=VMEM)
    sm = pl.BlockSpec(memory_space=SMEM)
    hbm = pl.BlockSpec(memory_space=pl.ANY)
    shape = jax.ShapeDtypeStruct

    table = jnp.concatenate(
        [sep_index, sep_owner, jnp.zeros((1, 2048 - bound - halves), jnp.int32)], axis=1
    )
    every_index = lax.all_gather(table, ("row", "col"), axis=0, tiled=True)

    outgoing, inv_high, inv_low = call(
        forward_kernel,
        (
            shape((fronts, PAD, sources), BF16),
            shape((2, half, half), BF16),
            shape((2, half, half), BF16),
        ),
        (sep_owner, bound_count, front_factor, rhs, coupling),
        [
            VMEM((2, half, half), F32),
            VMEM((half, half), F32),
            VMEM((order, sources), F32),
            VMEM((bound, order), BF16),
            VMEM((2, half, half), BF16),
            VMEM((2, half, half), BF16),
            VMEM((bound + 8, sources), F32),
            pltpu.SemaphoreType.DMA((7,)),
        ],
        [sm, sm, hbm, hbm, hbm],
        (vm, hbm, hbm),
        8_000_000_000,
        14_000_000,
        40,
    )
    incoming = lax.all_to_all(outgoing, ("row", "col"), split_axis=0, concat_axis=0, tiled=True)
    field0, g_high, g_low, s_high, s_low = call(
        prepare_kernel,
        (
            shape((cells, sources), F32),
            shape((cells, flat), BF16),
            shape((cells, flat), BF16),
            shape((sep_size, sep_size), BF16),
            shape((sep_size, sep_size), BF16),
        ),
        (
            sep_owner, bound_count, front_factor, rhs, coupling, inv_high, inv_low,
            cell_weight, cell_pivot, sep_factor,
        ),
        [
            VMEM((half, half), F32),
            VMEM((bound, order), BF16),
            VMEM((bound + 8, cells), F32),
            VMEM((fronts, PAD, cells), F32),
            pltpu.SemaphoreType.DMA((2,)),
        ],
        [sm, sm, hbm, vm, hbm, vm, vm, vm, vm, vm],
        (vm,) * 5,
        6_000_000_000,
        14_000_000,
        40,
    )
    me = (lax.axis_index("row") * col_count + lax.axis_index("col")).astype(jnp.int32).reshape(1)
    sel, sel_t = call(
        lambda *refs: select_kernel(*refs, bound=bound, halves=halves),
        (shape((sep_size, flat), BF16), shape((flat, sep_size), BF16)),
        (me, every_index),
        [],
        [sm, vm],
        (vm, vm),
        1_000_000_000,
        9_000_000,
        24,
    )
    sep_potential, replies = call(
        separator_kernel,
        (shape((sep_size, sources), F32), shape((flat, sources), BF16)),
        (sel, incoming.reshape(flat, sources), sep_rhs, s_high, s_low, sel_t),
        [],
        [vm] * 6,
        (vm, vm),
        3_000_000_000,
        13_000_000,
        32,
    )
    returned = lax.all_to_all(
        replies.reshape(fronts, PAD, sources),
        ("row", "col"),
        split_axis=0,
        concat_axis=0,
        tiled=True,
    ).reshape(flat, sources)
    field = call(
        field_kernel,
        shape((cells, sources), BF16),
        (field0, g_high, g_low, returned),
        [],
        [vm] * 4,
        vm,
        600_000_000,
        5_000_000,
        16,
    )
    row_tile = lax.all_gather(field, "col", axis=0, tiled=True)
    col_tile = lax.all_to_all(
        jnp.broadcast_to(field[None], (row_count, cells, sources)),
        "row",
        split_axis=0,
        concat_axis=0,
        tiled=True,
    ).reshape(row_count * cells, sources)
    gram = mm(row_tile, col_tile, NT) * (1.0 / sources)
    return (sep_potential, gram * gram)


def solution(mesh):
    placed = P(("row", "col"), None)
    return jax.shard_map(
        local,
        mesh=mesh,
        in_specs=(placed, placed, placed, P(("row", "col"))) + (placed,) * 6,
        out_specs=(placed, P("row", "col")),
        check_vma=False,
    )
```

time: 389 us -> 182 us (0.47); the launches traced: 383 us -> 181 us
  other arithmetic: 129 us -> 0 us
  waiting for transfers between devices: 93 us -> 25.7 us
  blocking collectives: 0 us -> 49.5 us
  matrix products: 50 us -> 4.69 us
  Pallas kernels: 0 us -> 37.2 us
  local copies, waits for them, and re-layouts: 63.8 us -> 34.6 us
  starting transfers between devices: 30.7 us -> 14.8 us
    another operation x8 -> x0, other arithmetic: 126 us -> none  [front_solve(): jax.scipy.linalg.solve_triangular(factor, half_way, trans=1, lower=True)]
    all_gather x1, waiting for transfers between devices: 65.6 us -> 21.2 us  [local(): every_index = lax.all_gather(table, ('row', 'col'), axis=0, tiled=True)]
    pallas_call x0 -> x5, Pallas kernels: none -> 37.2 us  [call(): pl.pallas_call(kernel, out_shape=outs, in_specs=specs, out_specs=out_spec...]
    all_to_all x0 -> x1, blocking collectives: none -> 36.4 us  [local(): lax.all_to_all(replies.reshape(fronts, PAD, sources), ('row', 'col'), spl...]
    another operation x47 -> x0, local copies, waits for them, and re-layouts: 36 us -> none  [the longest x34 24.2 us: front_solve(): jax.scipy.linalg.solve_triangular(factor, half_way, trans=1, lower=True)]
    another operation x74 -> x0, matrix products: 35.4 us -> none  [the longest x37 20.1 us: front_solve(): half_way = jax.scipy.linalg.solve_triangular(factor, right, lower=True)]
    unnamed x54 -> x55, local copies, waits for them, and re-layouts: 3.1 us -> 32.2 us
    all_to_all x2 -> x1, waiting for transfers between devices: 27.4 us -> 4.51 us  [local(): lax.all_to_all(jnp.broadcast_to(field[None], (row_count, cells, sources))...]
  transfers between devices with their start and end apart: 4 -> 3, of which waited for: 2 -> 2; matrix products, arithmetic and copies ran while one was open for 50% -> 1% of each run, Pallas kernels for 0% -> 17%
where the time goes in v1:
time: 182 us; the launch traced here: 181 us
  blocking collectives  49.5 us (27%)
  Pallas kernels  37.2 us (20%)
  local copies, waits for them, and re-layouts  34.6 us (19%)
  waiting for transfers between devices  25.7 us (14%)
  starting transfers between devices  14.8 us (8%)
  between operations  14.8 us (8%)
  matrix products  4.69 us (3%)
    pallas_call x5, Pallas kernels, call(): pl.pallas_call(kernel, out_shape=outs, in_specs=specs, out_specs=out_spec...  37.2 us
    all_to_all x1, blocking collectives, local(): lax.all_to_all(replies.reshape(fronts, PAD, sources), ('row', 'col'), spl...  36.4 us
    unnamed x55, local copies, waits for them, and re-layouts  32.2 us
    all_gather x1, waiting for transfers between devices, local(): every_index = lax.all_gather(table, ('row', 'col'), axis=0, tiled=True)  21.2 us
    all_gather x1, blocking collectives, local(): row_tile = lax.all_gather(field, 'col', axis=0, tiled=True)  13.1 us
    all_to_all x1, starting transfers between devices, local(): lax.all_to_all(outgoing, ('row', 'col'), split_axis=0, concat_axis=0, til...  11.1 us
    dot_general x1, matrix products, mm(): return lax.dot_general(a, b, dims, preferred_element_type=F32)  4.69 us
    all_to_all x1, waiting for transfers between devices, local(): lax.all_to_all(jnp.broadcast_to(field[None], (row_count, cells, sources))...  4.51 us
  transfers between devices with their start and end apart: 3, of which 2 were waited for; matrix products, arithmetic and copies ran while one was open for 1% of the time, Pallas kernels for 17%

profile of v1, /device:TPU:0, one launch (start us, length us, event | category | flops | bytes accessed | tf_op | source)
XLA Modules:
  0.0 181.3 jit_solution(11368172794422075076)
XLA Ops:
  7.2 1.4 concatenate.3
  9.9 2.2 %copy-done.14 = f32[1024,1024]{1,0:T(8,128)S(1)} copy-done((f32[1024,1024]{1,0:T(8,128)S(1)}, f32[1024,1024]{1,0:T(8,128)}, u32[]{:S(2)}) %copy-start.14) | copy-done | bytes 4194328
  12.1 2.0 %copy-done.15 = bf16[1792,1024]{1,0:T(8,128)(2,1)S(1)} copy-done((bf16[1792,1024]{1,0:T(8,128)(2,1)S(1)}, bf16[1792,1024]{1,0:T(8,128)(2,1)}, u32[]{:S(2)}) %copy-start.15) | copy-done | bytes 3670040
  14.2 1.2 copy-done.17
  15.4 13.7 %shard_map.114 = (bf16[128,32,256]{2,1,0:T(8,128)(2,1)S(1)}, bf16[2,512,512]{2,1,0:T(8,128)(2,1)S(1)}, bf16[2,512,512]{2,1,0:T(8,128)(2,1)S(1)}) custom-call(s32[1,64]{1,0:T(1,128)S(1)} %copy-done.12, s32[1]{0:T(128)S(6)} %copy.19.count_ref, f32[1024,1024]{1,0:T(8,128)S(1)} %copy-done.14, f32[1024,256]{1,0:T(8,128)S(1)} %copy-done.17, ...), custom_call_target="tpu_custom_call" | custom-call | flops 8000000000 | bytes 14000000 | tf_op jit(solution)/shard_map/pallas_call | solution.py:246
  29.1 1.4 copy-done.4
  30.5 1.0 copy-done.20
  31.4 1.0 copy-done.22
  32.4 11.1 %all-to-all-start = ((bf16[128,32,256]{2,1,0:T(8,128)(2,1)}), bf16[128,32,256]{2,1,0:T(8,128)(2,1)S(1)}, u32[]{:S(2)}, u32[]{:S(2)}) async-start(bf16[128,32,256]{2,1,0:T(8,128)(2,1)} %copy-done.4), calls=%async_computation | async-start | bytes 4194304 | tf_op jit(solution)/shard_map/all_to_all | solution.py:305
  43.8 2.0 %copy-done.16 = bf16[1792,1024]{1,0:T(8,128)(2,1)S(1)} copy-done((bf16[1792,1024]{1,0:T(8,128)(2,1)S(1)}, bf16[1792,1024]{1,0:T(8,128)(2,1)}, u32[]{:S(2)}) %copy-start.16) | copy-done | bytes 3670040
  45.8 1.2 copy-done.18
  47.0 1.2 copy-done.19
  48.3 1.2 copy-done.21
  49.5 1.2 copy-done.23
  50.7 13.5 %shard_map.115 = (f32[128,256]{1,0:T(8,128)S(1)}, bf16[128,4096]{1,0:T(8,128)(2,1)S(1)}, bf16[128,4096]{1,0:T(8,128)(2,1)S(1)}, bf16[512,512]{1,0:T(8,128)(2,1)S(1)}, bf16[512,512]{1,0:T(8,128)(2,1)S(1)}) custom-call(s32[1,64]{1,0:T(1,128)S(1)} %copy-done.13, s32[1]{0:T(128)S(6)} %copy.19.count_ref, f32[1024,1024]{1,0:T(8,128)} %factor.3, ...), custom_call_target="tpu_custom_call" | custom-call | flops 6000000000 | bytes 14000000 | tf_op jit(solution)/shard_map/pallas_call | solution.py:246
  66.8 21.2 %all-gather.3.cloned.1.call-done = s32[128,1,2048]{2,1,0:T(1,128)} async-done(((s32[1,1,2048]{2,1,0:T(1,128)}), s32[128,1,2048]{2,1,0:T(1,128)}) %all-gather.3.cloned.1.call-update) | async-done | bytes 1048592 | tf_op jit(solution)/shard_map/all_gather | solution.py:279
  88.0 1.6 copy.18
  89.5 4.3 %shard_map.113 = (bf16[512,4096]{1,0:T(8,128)(2,1)S(1)}, bf16[4096,512]{1,0:T(8,128)(2,1)S(1)}) custom-call(s32[1]{0:T(128)} %bitcast.refs_0_, s32[128,2048]{1,0:T(8,128)S(1)} %bitcast.14), custom_call_target="tpu_custom_call" | custom-call | flops 1000000000 | bytes 9000000 | tf_op jit(solution)/shard_map/pallas_call | solution.py:246
  93.8 2.0 %copy-done = bf16[512,4096]{1,0:T(8,128)(2,1)} copy-done((bf16[512,4096]{1,0:T(8,128)(2,1)}, bf16[512,4096]{1,0:T(8,128)(2,1)S(1)}, u32[]{:S(2)}) %copy-start) | copy-done | bytes 4194328
  95.9 2.0 %copy-done.2 = bf16[4096,512]{1,0:T(8,128)(2,1)} copy-done((bf16[4096,512]{1,0:T(8,128)(2,1)}, bf16[4096,512]{1,0:T(8,128)(2,1)S(1)}, u32[]{:S(2)}) %copy-start.2) | copy-done | bytes 4194328
  97.8 2.2 %copy-done.1 = bf16[512,4096]{1,0:T(8,128)(2,1)S(1)} copy-done((bf16[512,4096]{1,0:T(8,128)(2,1)S(1)}, bf16[512,4096]{1,0:T(8,128)(2,1)}, u32[]{:S(2)}) %copy-start.1) | copy-done | bytes 4194328
  100.0 2.2 %copy-done.3 = bf16[4096,512]{1,0:T(8,128)(2,1)S(1)} copy-done((bf16[4096,512]{1,0:T(8,128)(2,1)S(1)}, bf16[4096,512]{1,0:T(8,128)(2,1)}, u32[]{:S(2)}) %copy-start.3) | copy-done | bytes 4194328
  102.2 1.0 copy-done.7
  103.2 1.0 copy-done.9
  104.3 1.0 copy-done.11
  105.3 5.0 %shard_map.116 = (f32[512,256]{1,0:T(8,128)}, bf16[4096,256]{1,0:T(8,128)(2,1)S(1)}) custom-call(bf16[512,4096]{1,0:T(8,128)(2,1)S(1)} %copy-done.1, bf16[4096,256]{1,0:T(8,128)(2,1)S(1)} %bitcast.12, f32[512,256]{1,0:T(8,128)S(1)} %copy-done.7, bf16[512,512]{1,0:T(8,128)(2,1)S(1)} %copy-done.9, bf16[512,512]{1,0:T(8,128)(2,1)S(1)} %copy-done.11, ...), custom_call_target="tpu_custom_call" | custom-call | flops 3000000000 | bytes 13000000 | tf_op jit(solution)/shard_map/pallas_call | solution.py:246
  110.3 36.4 %all_to_all.15 = bf16[128,32,256]{2,1,0:T(8,128)(2,1)S(1)} all-to-all(bf16[128,32,256]{2,1,0:T(8,128)(2,1)S(1)} %bitcast.13), channel_id=1, replica_groups=mesh['row'=16,'col'=8] {'row','col'}, dimensions={0} | all-to-all | bytes 4194304 | tf_op jit(solution)/shard_map/all_to_all | solution.py:355
  147.4 1.1 broadcast_in_dim.10
  148.5 3.7 %all-to-all-start.2 = ((bf16[16,128,256]{2,1,0:T(8,128)(2,1)}), bf16[16,128,256]{2,1,0:T(8,128)(2,1)S(1)}, u32[]{:S(2)}, u32[]{:S(2)}) async-start(bf16[16,128,256]{2,1,0:T(8,128)(2,1)} %broadcast_in_dim.10), calls=%async_computation.2 | async-start | bytes 2097152 | tf_op jit(solution)/shard_map/all_to_all | solution.py:374
  152.2 13.1 %all_gather.7 = bf16[1024,256]{1,0:T(8,128)(2,1)S(1)} all-gather(bf16[128,256]{1,0:T(8,128)(2,1)S(1)} %shard_map.117), channel_id=1, replica_groups=mesh['row'=16,'col'=8] {'col'}, dimensions={0}, use_global_device_ids=true | all-gather | bytes 589824 | tf_op jit(solution)/shard_map/all_gather | solution.py:373
  165.3 4.5 %all-to-all-done.2 = bf16[16,128,256]{2,1,0:T(8,128)(2,1)S(1)} async-done(((bf16[16,128,256]{2,1,0:T(8,128)(2,1)}), bf16[16,128,256]{2,1,0:T(8,128)(2,1)S(1)}, u32[]{:S(2)}, u32[]{:S(2)}) %all-to-all-start.2) | async-done | bytes 1048608 | tf_op jit(solution)/shard_map/all_to_all | solution.py:374
  169.8 4.7 %multiply_multiply_fusion = f32[1024,2048]{1,0:T(8,128)} fusion(bf16[1024,256]{1,0:T(8,128)(2,1)S(1)} %all_gather.7, bf16[2048,256]{1,0:T(8,128)(2,1)S(1)} %bitcast.15), kind=kOutput, calls=%fused_computation | convolution fusion | flops 1077936128 | bytes 9961472 | tf_op jit(solution)/shard_map/dot_general | solution.py:20
  (41 shorter events, 4.3 us)
Async XLA Ops:
  7.2 80.8 %all-gather.3.cloned.1.call-start = ((), (), s32[]{:S(2)}) async-start(), calls=%async_computation.3 | async-start | bytes 1056768 | tf_op jit(solution)/shard_map/all_gather | solution.py:279
  9.3 0.7 copy-start.12
  9.9 2.2 %copy-start.14 = (f32[1024,1024]{1,0:T(8,128)S(1)}, f32[1024,1024]{1,0:T(8,128)}, u32[]{:S(2)}) copy-start(f32[1024,1024]{1,0:T(8,128)} %factor.3) | copy-start | bytes 12582916
  12.1 2.0 %copy-start.15 = (bf16[1792,1024]{1,0:T(8,128)(2,1)S(1)}, bf16[1792,1024]{1,0:T(8,128)(2,1)}, u32[]{:S(2)}) copy-start(bf16[1792,1024]{1,0:T(8,128)(2,1)} %coupling.3) | copy-start | bytes 11010052
  14.2 1.2 copy-start.17
  29.1 1.4 copy-start.4
  30.5 1.0 copy-start.20
  31.4 1.0 copy-start.22
  32.4 11.2 %copy-start.24 = (f32[128,8]{0,1:T(8,128)S(1)}, f32[128,8]{0,1:T(8,128)}, u32[]{:S(2)}) copy-start(f32[128,8]{0,1:T(8,128)} %param.18) | copy-start | bytes 12292
  32.4 11.3 %copy-start.25 = (s32[128,8]{0,1:T(8,128)S(1)}, s32[128,8]{0,1:T(8,128)}, u32[]{:S(2)}) copy-start(s32[128,8]{0,1:T(8,128)} %param.19) | copy-start | bytes 12292
  32.4 11.4 %copy-start.13 = (s32[1,64]{1,0:T(1,128)S(1)}, s32[1,64]{1,0:T(1,128)}, u32[]{:S(2)}) copy-start(s32[1,64]{1,0:T(1,128)} %owner_ref.3) | copy-start | bytes 772
  32.4 65.4 %all-to-all-start = ((bf16[128,32,256]{2,1,0:T(8,128)(2,1)}), bf16[128,32,256]{2,1,0:T(8,128)(2,1)S(1)}, u32[]{:S(2)}, u32[]{:S(2)}) async-start(bf16[128,32,256]{2,1,0:T(8,128)(2,1)} %copy-done.4), calls=%async_computation | async-start | bytes 4194304 | tf_op jit(solution)/shard_map/all_to_all | solution.py:305
  43.8 2.0 %copy-start.16 = (bf16[1792,1024]{1,0:T(8,128)(2,1)S(1)}, bf16[1792,1024]{1,0:T(8,128)(2,1)}, u32[]{:S(2)}) copy-start(bf16[1792,1024]{1,0:T(8,128)(2,1)} %coupling.3) | copy-start | bytes 11010052
  45.8 1.2 copy-start.18
  47.0 1.2 copy-start.19
  48.3 1.2 copy-start.21
  49.5 1.2 copy-start.23
  64.2 1.0 copy-start.5
  65.2 0.8 copy-start.8
  66.0 0.8 copy-start.10
  93.8 2.0 %copy-start = (bf16[512,4096]{1,0:T(8,128)(2,1)}, bf16[512,4096]{1,0:T(8,128)(2,1)S(1)}, u32[]{:S(2)}) copy-start(bf16[512,4096]{1,0:T(8,128)(2,1)S(1)} %get-tuple-element.14.sel) | copy-start | bytes 12582916
  95.9 2.0 %copy-start.2 = (bf16[4096,512]{1,0:T(8,128)(2,1)}, bf16[4096,512]{1,0:T(8,128)(2,1)S(1)}, u32[]{:S(2)}) copy-start(bf16[4096,512]{1,0:T(8,128)(2,1)S(1)} %get-tuple-element.20.sel_t) | copy-start | bytes 12582916
  97.8 2.2 %copy-start.1 = (bf16[512,4096]{1,0:T(8,128)(2,1)S(1)}, bf16[512,4096]{1,0:T(8,128)(2,1)}, u32[]{:S(2)}) copy-start(bf16[512,4096]{1,0:T(8,128)(2,1)} %copy-done) | copy-start | bytes 12582916
  100.0 2.2 %copy-start.3 = (bf16[4096,512]{1,0:T(8,128)(2,1)S(1)}, bf16[4096,512]{1,0:T(8,128)(2,1)}, u32[]{:S(2)}) copy-start(bf16[4096,512]{1,0:T(8,128)(2,1)} %copy-done.2) | copy-start | bytes 12582916
  102.2 1.0 copy-start.7
  103.2 1.0 copy-start.9
  104.3 1.0 copy-start.11
  110.3 36.4 %copy-start.6 = (bf16[128,4096]{1,0:T(8,128)(2,1)S(1)}, bf16[128,4096]{1,0:T(8,128)(2,1)}, u32[]{:S(2)}) copy-start(bf16[128,4096]{1,0:T(8,128)(2,1)} %copy-done.5) | copy-start | bytes 3145732
  148.5 21.3 %all-to-all-start.2 = ((bf16[16,128,256]{2,1,0:T(8,128)(2,1)}), bf16[16,128,256]{2,1,0:T(8,128)(2,1)S(1)}, u32[]{:S(2)}, u32[]{:S(2)}) async-start(bf16[16,128,256]{2,1,0:T(8,128)(2,1)} %broadcast_in_dim.10), calls=%async_computation.2 | async-start | bytes 2097152 | tf_op jit(solution)/shard_map/all_to_all | solution.py:374
Sparse Core Ops, SparseCore 0:
  10.8 77.1 all-gather.2

commit v2 on v1

v2 whole, which is shorter than its diff:
```python
import jax
import jax.numpy as jnp
from jax import lax
from jax.experimental import pallas as pl
from jax.experimental.pallas import tpu as pltpu
from jax.sharding import PartitionSpec as P

F32 = jnp.float32
BF16 = jnp.bfloat16
NN = (((1,), (0,)), ((), ()))
NT = (((1,), (1,)), ((), ()))
UNIT = 128
BASE = 256
WIDE = 512
PAD = 32
LANES = 128
VMEM = pltpu.VMEM
SMEM = pltpu.SMEM


def mm(a, b, dims=NN):
    return lax.dot_general(a, b, dims, preferred_element_type=F32)


def split(x):
    high = x.astype(BF16)
    return high, (x - high.astype(F32)).astype(BF16)


def mm3(a, b, dims=NN):
    return mm(a[0], b[0], dims) + (mm(a[0], b[1], dims) + mm(a[1], b[0], dims))


def side_by_side(first, second):
    return jnp.concatenate([first, second], axis=1)


def on_diagonal(pair):
    order = pair.shape[0]
    zero = jnp.zeros((order, order), pair.dtype)
    return jnp.concatenate(
        [side_by_side(pair[:, :order], zero), side_by_side(zero, pair[:, order:])], axis=0
    )


def mm_pair(a, b):
    return mm3(a, (on_diagonal(b[0]), on_diagonal(b[1])))


def invert_lower(read, count):
    row = lax.broadcasted_iota(jnp.int32, (UNIT, 2 * UNIT), 0)
    col = lax.broadcasted_iota(jnp.int32, (UNIT, 2 * UNIT), 1) & (UNIT - 1)
    first = lax.broadcasted_iota(jnp.int32, (UNIT, 2 * UNIT), 1) < UNIT

    def below(level):
        same = (row >> (level + 1)) == (col >> (level + 1))
        return same & (((row >> level) & 1) == 1) & (((col >> level) & 1) == 0)

    pairs = [side_by_side(read(b, 0, 0), read(b, 1, 1)) for b in range(count)]
    found = []
    mask = below(0)
    for pair in pairs:
        diagonal = jnp.where(row == col, pair, 0.0)
        across = 1.0 / jnp.where(row == col, pair, 1.0)
        across = jnp.sum(jnp.where(row == col, across, 0.0), axis=0, keepdims=True)
        down = 1.0 / jnp.where(
            first,
            jnp.sum(diagonal[:, :UNIT], axis=1, keepdims=True),
            jnp.sum(diagonal[:, UNIT:], axis=1, keepdims=True),
        )
        below_it = jnp.where(mask, -(down * pair * across), 0.0)
        found.append(jnp.where(row == col, down, below_it))
    level = 1
    while (1 << level) < UNIT:
        mask = below(level)
        parts = [split(one) for one in found]
        halves = [mm_pair(p, split(jnp.where(mask, pair, 0.0))) for p, pair in zip(parts, pairs)]
        found = [one - mm_pair(split(h), p) for one, h, p in zip(found, halves, parts)]
        level += 1
    result = []
    for b in range(0, count, 2):
        left, right = found[b], found[b + 1]
        tops = split(side_by_side(left[:, :UNIT], right[:, :UNIT]))
        ends = split(side_by_side(left[:, UNIT:], right[:, UNIT:]))
        between = split(side_by_side(read(b, 1, 0), read(b + 1, 1, 0)))
        corners = -mm_pair(ends, split(mm_pair(between, tops)))
        zero = jnp.zeros((UNIT, UNIT), F32)
        for k, one in enumerate((left, right)):
            corner = corners[:, k * UNIT : (k + 1) * UNIT]
            result.append(
                jnp.concatenate(
                    [side_by_side(one[:, :UNIT], zero), side_by_side(corner, one[:, UNIT:])], axis=0
                )
            )
    return result


def place_rows(source, target, owner_ref, count, slots, halves, extra=None):
    width = target.shape[2]
    row = lax.broadcasted_iota(jnp.int32, (PAD, width), 0)
    for j in range(halves):
        live = jnp.minimum(count - slots * j, slots)
        rows = source[slots * j : slots * j + PAD, :]
        rows = jnp.where(row < live, rows, 0.0)
        if extra is not None:
            rows = jnp.where(row == slots, extra[j : j + 1, :], rows)
        target[owner_ref[0, j]] = rows.astype(target.dtype)


def one_hot(cond):
    return jnp.where(cond, 1.0, 0.0).astype(BF16)


def group_of(row):
    return (row * 2341) >> 16


def forward_kernel(
    owner_ref, count_ref, me_ref, index, factor, rhs, coupling,
    out_hbm, high_out, low_out,
    diag, lower, right, block, high, low, contrib, out, sems,
):
    half = diag.shape[1]
    bound = coupling.shape[0]
    halves = owner_ref.shape[1]
    slots = bound // halves
    copies = [
        pltpu.make_async_copy(factor.at[0:half, 0:half], diag.at[0], sems.at[0]),
        pltpu.make_async_copy(factor.at[half : 2 * half, half : 2 * half], diag.at[1], sems.at[1]),
        pltpu.make_async_copy(rhs, right, sems.at[2]),
        pltpu.make_async_copy(factor.at[half : 2 * half, 0:half], lower, sems.at[3]),
        pltpu.make_async_copy(coupling, block, sems.at[4]),
    ]
    for copy in copies:
        copy.start()
    out[...] = jnp.zeros_like(out)
    contrib[bound:, :] = jnp.zeros((contrib.shape[0] - bound, contrib.shape[1]), F32)
    mine = group_of(lax.broadcasted_iota(jnp.int32, (halves, bound), 1)) == (
        lax.broadcasted_iota(jnp.int32, (halves, bound), 0)
    )
    values = index[...]
    low_bits = jnp.where(mine, (values & 255).astype(F32), 0.0).astype(BF16)
    high_bits = jnp.where(mine, ((values >> 8) + 1).astype(F32), 0.0).astype(BF16)
    at = lax.broadcasted_iota(jnp.int32, (bound, LANES), 0)
    lane = lax.broadcasted_iota(jnp.int32, (bound, LANES), 1)
    part = me_ref[0] & (LANES // PAD - 1)
    fold = one_hot((at - slots * group_of(at)) + PAD * part == lane)
    extra = side_by_side(mm(low_bits, fold), mm(high_bits, fold))
    copies[0].wait()
    copies[1].wait()

    def read(b, i, k):
        top = (b % 2) * BASE
        return diag[
            b // 2, top + i * UNIT : top + (i + 1) * UNIT, top + k * UNIT : top + (k + 1) * UNIT
        ]

    inverses = invert_lower(read, 4)
    for i in range(2):
        first_parts, second_parts = split(inverses[2 * i]), split(inverses[2 * i + 1])
        between = split(diag[i, BASE:, :BASE])
        corner = split(-mm3(second_parts, split(mm3(between, first_parts))))
        for k, ref in enumerate((high, low)):
            ref[i, :BASE, :BASE] = first_parts[k]
            ref[i, BASE:, BASE:] = second_parts[k]
            ref[i, BASE:, :BASE] = corner[k]
            ref[i, :BASE, BASE:] = jnp.zeros((BASE, BASE), BF16)
    keep = [
        pltpu.make_async_copy(high, high_out, sems.at[5]),
        pltpu.make_async_copy(low, low_out, sems.at[6]),
    ]
    for copy in keep:
        copy.start()
    copies[2].wait()
    copies[3].wait()
    inv = [(high[i], low[i]) for i in range(2)]
    off = split(lower[...])
    turned = right[...].T
    x0 = mm3(split(turned[:, :half]), inv[0], NT)
    x1 = mm3(split(turned[:, half:] - mm3(split(x0), off, NT)), inv[1], NT)
    y1 = mm3(split(x1), inv[1])
    y0 = mm3(split(x0 - mm3(split(y1), off)), inv[0])
    copies[4].wait()
    contrib[:bound, :] = mm(block[:, :half], y0.astype(BF16), NT) + mm(
        block[:, half:], y1.astype(BF16), NT
    )
    place_rows(contrib, out, owner_ref, count_ref[0], slots, halves, extra)
    keep.append(pltpu.make_async_copy(out, out_hbm, sems.at[0]))
    keep[-1].start()
    for copy in keep:
        copy.wait()


def schur_kernel(sep_hbm, s_high, s_low, sep, sem):
    copy = pltpu.make_async_copy(sep_hbm, sep, sem)
    copy.start()
    copy.wait()

    def read(b, i, k):
        top = b * BASE
        return sep[top + i * UNIT : top + (i + 1) * UNIT, top + k * UNIT : top + (k + 1) * UNIT]

    first, second = invert_lower(read, 2)
    first_parts, second_parts = split(first), split(second)
    corner = -mm3(second_parts, split(mm3(split(sep[BASE:, :BASE]), first_parts)))
    corner_parts = split(corner)
    first_t, second_t, corner_t = split(first.T), split(second.T), split(corner.T)
    pieces = (
        (0, 0, mm3(first_t, first_parts) + mm3(corner_t, corner_parts)),
        (0, 1, mm3(corner_t, second_parts)),
        (1, 0, mm3(second_t, corner_parts)),
        (1, 1, mm3(second_t, second_parts)),
    )
    for i, k, piece in pieces:
        at = (slice(i * BASE, (i + 1) * BASE), slice(k * BASE, (k + 1) * BASE))
        s_high[at], s_low[at] = split(piece)


def project_kernel(
    owner_ref, count_ref, factor, rhs, coupling, high_hbm, low_hbm, weight, pivot,
    field0, g_high, g_low,
    lower, right, block, high, low, rows, placed, sems,
):
    half = lower.shape[0]
    bound = coupling.shape[0]
    halves = owner_ref.shape[1]
    cells = weight.shape[0]
    copies = [
        pltpu.make_async_copy(high_hbm, high, sems.at[0]),
        pltpu.make_async_copy(low_hbm, low, sems.at[1]),
        pltpu.make_async_copy(factor.at[half : 2 * half, 0:half], lower, sems.at[2]),
        pltpu.make_async_copy(rhs, right, sems.at[3]),
        pltpu.make_async_copy(coupling, block, sems.at[4]),
    ]
    for copy in copies:
        copy.start()
    placed[...] = jnp.zeros_like(placed)
    places = lax.broadcasted_iota(jnp.int32, (cells, 2 * half), 1)
    project = jnp.zeros((cells, 2 * half), F32)
    for k in range(weight.shape[1]):
        project += jnp.where(places == pivot[:, k : k + 1], weight[:, k : k + 1], 0.0)
    for copy in copies[:3]:
        copy.wait()
    inv = [(high[i], low[i]) for i in range(2)]
    off = split(lower[...])
    x0 = mm3(split(project[:, :half]), inv[0], NT)
    x1 = mm3(split(project[:, half:] - mm3(split(x0), off, NT)), inv[1], NT)
    y1 = mm3(split(x1), inv[1])
    y0 = mm3(split(x0 - mm3(split(y1), off)), inv[0])
    y0, y1 = split(y0), split(y1)
    copies[3].wait()
    field0[...] = mm3(y0, split(right[:half, :])) + mm3(y1, split(right[half:, :]))
    copies[4].wait()
    both = mm(block[:, :half], jnp.concatenate(y0, axis=0), NT) + mm(
        block[:, half:], jnp.concatenate(y1, axis=0), NT
    )
    rows[:bound, :] = both[:, :cells] + both[:, cells:]
    rows[bound:, :] = jnp.zeros((rows.shape[0] - bound, cells), F32)
    place_rows(rows, placed, owner_ref, count_ref[0], bound // halves, halves)
    group = LANES // PAD
    for t in range(placed.shape[0] // group):
        tile = placed[t * group : (t + 1) * group].reshape(LANES, cells).T
        g_high[:, t * LANES : (t + 1) * LANES], g_low[:, t * LANES : (t + 1) * LANES] = split(tile)


def pick(cond):
    return jnp.where(cond, jnp.ones((), BF16), jnp.zeros((), BF16))


def separator_kernel(
    incoming, rhs_hbm, high_hbm, low_hbm, potential, replies, right, high, low, sems, *, fronts, slots
):
    copies = [
        pltpu.make_async_copy(source, target, sems.at[k])
        for k, (source, target) in enumerate(((rhs_hbm, right), (high_hbm, high), (low_hbm, low)))
    ]
    for copy in copies:
        copy.start()
    group = LANES // PAD
    tail = incoming[...].reshape(fronts, PAD, -1)[:, PAD - 8 :, :].astype(F32)
    tail = tail.reshape(fronts // group, group, 8, -1)
    tail = (tail[:, 0] + tail[:, 1]) + (tail[:, 2] + tail[:, 3])
    tail = tail[:, slots - (PAD - 8), :]
    low_bits, high_bits = tail[:, :LANES], tail[:, LANES:]
    rows = [jnp.where(high_bits == 1.0 + p, low_bits, -1.0) for p in range(2)]
    empty = jnp.full((LANES - rows[0].shape[0], LANES), -1.0, F32)
    cols = [jnp.concatenate([one, empty], axis=0).T for one in rows]
    part = right.shape[0] // 2
    down = lax.broadcasted_iota(jnp.int32, (part, LANES), 0).astype(F32).astype(BF16)
    along = lax.broadcasted_iota(jnp.int32, (LANES, part), 1).astype(F32).astype(BF16)
    groups = incoming.shape[0] // LANES
    each = WIDE // LANES
    total = None
    for c in range(groups // each):
        tiles = [
            jnp.concatenate(
                [pick(down == rows[p][g : g + 1, :].astype(BF16)) for p in range(2)], axis=0
            )
            for g in range(c * each, (c + 1) * each)
        ]
        term = mm(jnp.concatenate(tiles, axis=1), incoming[c * WIDE : (c + 1) * WIDE, :])
        total = term if total is None else total + term
    for copy in copies:
        copy.wait()
    found = mm3((high[...], low[...]), split(right[...] - total))
    potential[...] = found
    rounded = found.astype(BF16)
    for c in range(groups // each):
        tiles = [
            jnp.concatenate(
                [pick(along == cols[p][:, g : g + 1].astype(BF16)) for p in range(2)], axis=1
            )
            for g in range(c * each, (c + 1) * each)
        ]
        chosen = jnp.concatenate(tiles, axis=0)
        replies[c * WIDE : (c + 1) * WIDE, :] = mm(chosen, rounded).astype(BF16)


def field_kernel(field0, g_high, g_low, returned, field, spread):
    values = returned[...]
    found = (field0[...] - (mm(g_high[...], values) + mm(g_low[...], values))).astype(BF16)
    field[...] = found
    for r in range(spread.shape[0]):
        spread[r] = found


def hess_kernel(me_ref, pair, *refs):
    others, col_tile, hess = refs[:-5], refs[-5], refs[-4]
    row_tile, tiles, sems = refs[-3:]
    scale = 1.0 / col_tile.shape[1]
    me = me_ref[0]
    for d, block in enumerate((pair,) + others):
        row_tile[me ^ (2 * d)] = block[0]
        row_tile[me ^ (2 * d + 1)] = block[1]
    rows = row_tile[...].reshape(-1, col_tile.shape[1])
    slots, _, width = tiles.shape
    copies = []
    for t in range(hess.shape[1] // width):
        slot = t % slots
        if t >= slots:
            copies[t - slots].wait()
        gram = mm(rows, col_tile[t * width : (t + 1) * width, :], NT) * scale
        tiles[slot] = gram * gram
        copies.append(
            pltpu.make_async_copy(
                tiles.at[slot], hess.at[:, t * width : (t + 1) * width], sems.at[slot]
            )
        )
        copies[-1].start()
    for copy in copies[-slots:]:
        copy.wait()


def call(kernel, outs, ins, scratch, specs, out_specs, flops, moved, vmem):
    return pl.pallas_call(
        kernel,
        out_shape=outs,
        in_specs=specs,
        out_specs=out_specs,
        scratch_shapes=scratch,
        compiler_params=pltpu.CompilerParams(vmem_limit_bytes=vmem * 1024 * 1024),
        cost_estimate=pl.CostEstimate(flops=flops, bytes_accessed=moved, transcendentals=0),
    )(*ins)


def local(
    rhs, front_factor, coupling, bound_count, sep_owner, sep_index, sep_rhs, sep_factor,
    cell_weight, cell_pivot,
):
    row_count = lax.axis_size("row")
    col_count = lax.axis_size("col")
    fronts = row_count * col_count
    bound, order = coupling.shape
    sources = rhs.shape[1]
    sep_size = sep_rhs.shape[0]
    halves = sep_owner.shape[1]
    cells = cell_weight.shape[0]
    half = order // 2
    flat = fronts * PAD
    vm = pl.BlockSpec(memory_space=VMEM)
    sm = pl.BlockSpec(memory_space=SMEM)
    hbm = pl.BlockSpec(memory_space=pl.ANY)
    shape = jax.ShapeDtypeStruct

    dma = pltpu.SemaphoreType.DMA
    both = ("row", "col")
    me = lax.axis_index("col").astype(jnp.int32).reshape(1)
    outgoing, inv_high, inv_low = call(
        forward_kernel,
        (
            shape((fronts, PAD, sources), BF16),
            shape((2, half, half), BF16),
            shape((2, half, half), BF16),
        ),
        (sep_owner, bound_count, me, sep_index, front_factor, rhs, coupling),
        [
            VMEM((2, half, half), F32),
            VMEM((half, half), F32),
            VMEM((order, sources), F32),
            VMEM((bound, order), BF16),
            VMEM((2, half, half), BF16),
            VMEM((2, half, half), BF16),
            VMEM((bound + 8, sources), F32),
            VMEM((fronts, PAD, sources), BF16),
            dma((7,)),
        ],
        [sm, sm, sm, vm, hbm, hbm, hbm],
        (hbm,) * 3,
        8_000_000_000,
        14_000_000,
        58,
    )

    def exchange(blocks):
        return lax.all_to_all(
            blocks.reshape(fronts, PAD, sources), both, split_axis=0, concat_axis=0, tiled=True
        ).reshape(flat, sources)

    incoming = exchange(outgoing)
    s_high, s_low = call(
        schur_kernel,
        (shape((sep_size, sep_size), BF16), shape((sep_size, sep_size), BF16)),
        (sep_factor,),
        [VMEM((sep_size, sep_size), F32), dma],
        [hbm],
        (vm, vm),
        2_000_000_000,
        3_000_000,
        24,
    )
    sep_potential, replies = call(
        lambda *refs: separator_kernel(*refs, fronts=fronts, slots=bound // halves),
        (shape((sep_size, sources), F32), shape((flat, sources), BF16)),
        (incoming, sep_rhs, s_high, s_low),
        [
            VMEM((sep_size, sources), F32),
            VMEM((sep_size, sep_size), BF16),
            VMEM((sep_size, sep_size), BF16),
            dma((3,)),
        ],
        [vm, hbm, hbm, hbm],
        (vm, vm),
        3_000_000_000,
        5_000_000,
        28,
    )
    returned = exchange(replies)
    weight, _ = lax.optimization_barrier((cell_weight, sep_potential))
    field0, g_high, g_low = call(
        project_kernel,
        (
            shape((cells, sources), F32),
            shape((cells, flat), BF16),
            shape((cells, flat), BF16),
        ),
        (
            sep_owner, bound_count, front_factor, rhs, coupling, inv_high, inv_low,
            weight, cell_pivot,
        ),
        [
            VMEM((half, half), F32),
            VMEM((order, sources), F32),
            VMEM((bound, order), BF16),
            VMEM((2, half, half), BF16),
            VMEM((2, half, half), BF16),
            VMEM((bound + 8, cells), F32),
            VMEM((fronts, PAD, cells), F32),
            dma((5,)),
        ],
        [sm, sm, hbm, hbm, hbm, hbm, hbm, vm, vm],
        (vm,) * 3,
        4_000_000_000,
        11_000_000,
        32,
    )
    field, spread = call(
        field_kernel,
        (shape((cells, sources), BF16), shape((row_count, cells, sources), BF16)),
        (field0, g_high, g_low, returned),
        [],
        [vm] * 4,
        (vm, vm),
        600_000_000,
        5_000_000,
        16,
    )
    col_tile = lax.all_to_all(
        spread, "row", split_axis=0, concat_axis=0, tiled=True
    ).reshape(row_count * cells, sources)
    mate = lax.ppermute(field, "col", [(i, i ^ 1) for i in range(col_count)])
    pair = jnp.stack([field, mate])
    others = [
        lax.ppermute(pair, "col", [(i, i ^ (2 * d)) for i in range(col_count)])
        for d in range(1, col_count // 2)
    ]
    hess = call(
        hess_kernel,
        shape((col_count * cells, row_count * cells), F32),
        (me, pair, *others, col_tile),
        [
            VMEM((col_count, cells, sources), BF16),
            VMEM((4, col_count * cells, BASE), F32),
            dma((4,)),
        ],
        [sm] + [vm] * (col_count // 2 + 1),
        hbm,
        1_000_000_000,
        10_000_000,
        24,
    )
    return (sep_potential, hess)


def solution(mesh):
    placed = P(("row", "col"), None)
    return jax.shard_map(
        local,
        mesh=mesh,
        in_specs=(placed, placed, placed, P(("row", "col"))) + (placed,) * 6,
        out_specs=(placed, P("row", "col")),
        check_vma=False,
    )
```

time: 182 us -> 129 us (0.71)
  blocking collectives: 49.5 us -> 0 us
  waiting for transfers between devices: 25.7 us -> 51.1 us
  local copies, waits for them, and re-layouts: 34.6 us -> 16.4 us
  between operations: 14.8 us -> 1.6 us
  starting transfers between devices: 14.8 us -> 24.2 us
  matrix products: 4.69 us -> 0 us
  Pallas kernels: 37.2 us -> 35.2 us
    all_to_all x2 -> x3, waiting for transfers between devices: 4.52 us -> 43.7 us  [the longest x2 37.7 us: exchange(): lax.all_to_all(blocks.reshape(fronts, PAD, sources), both, split_axis=0,...]
    all_to_all x1 -> x0, blocking collectives: 36.4 us -> none  [local(): lax.all_to_all(replies.reshape(fronts, PAD, sources), ('row', 'col'), spl...]
    all_gather x1 -> x0, waiting for transfers between devices: 21.2 us -> none  [local(): every_index = lax.all_gather(table, ('row', 'col'), axis=0, tiled=True)]
    unnamed x55 -> x35, local copies, waits for them, and re-layouts: 32.2 us -> 16.2 us
    all_gather x1 -> x0, blocking collectives: 13.1 us -> none  [local(): row_tile = lax.all_gather(field, 'col', axis=0, tiled=True)]
    ppermute x0 -> x4, waiting for transfers between devices: none -> 7.34 us  [the longest x3 6.1 us: local(): lax.ppermute(pair, 'col', [(i, i ^ 2 * d) for i in range(col_count)])]
    all_to_all x2 -> x3, starting transfers between devices: 14.8 us -> 20 us  [the longest x2 16.3 us: exchange(): lax.all_to_all(blocks.reshape(fronts, PAD, sources), both, split_axis=0,...]
    dot_general x1 -> x0, matrix products: 4.69 us -> none  [mm(): return lax.dot_general(a, b, dims, preferred_element_type=F32)]
  transfers between devices with their start and end apart: 3 -> 7, of which waited for: 2 -> 6; matrix products, arithmetic and copies ran while one was open for 1% -> 0% of each run, Pallas kernels for 17% -> 9%
where the time goes in v2:
time: 129 us; the launch traced here: 128 us
  waiting for transfers between devices  51.1 us (40%)
  Pallas kernels  35.2 us (27%)
  starting transfers between devices  24.2 us (19%)
  local copies, waits for them, and re-layouts  16.4 us (13%)
  between operations  1.6 us (1%)
    all_to_all x2, waiting for transfers between devices, exchange(): lax.all_to_all(blocks.reshape(fronts, PAD, sources), both, split_axis=0,...  37.7 us
    pallas_call x6, Pallas kernels, call(): pl.pallas_call(kernel, out_shape=outs, in_specs=specs, out_specs=out_spec...  35.2 us
    all_to_all x2, starting transfers between devices, exchange(): lax.all_to_all(blocks.reshape(fronts, PAD, sources), both, split_axis=0,...  16.3 us
    unnamed x35, local copies, waits for them, and re-layouts  16.2 us
    ppermute x3, waiting for transfers between devices, local(): lax.ppermute(pair, 'col', [(i, i ^ 2 * d) for i in range(col_count)])  6.1 us
    all_to_all x1, waiting for transfers between devices, local(): lax.all_to_all(spread, 'row', split_axis=0, concat_axis=0, tiled=True)  6.01 us
    ppermute x3, starting transfers between devices, local(): lax.ppermute(pair, 'col', [(i, i ^ 2 * d) for i in range(col_count)])  4.17 us
    all_to_all x1, starting transfers between devices, local(): lax.all_to_all(spread, 'row', split_axis=0, concat_axis=0, tiled=True)  3.66 us
  transfers between devices with their start and end apart: 7, of which 6 were waited for; matrix products, arithmetic and copies ran while one was open for 0% of the time, Pallas kernels for 9%

profile of v2, /device:TPU:0, one launch (start us, length us, event | category | flops | bytes accessed | tf_op | source)
XLA Modules:
  0.0 128.5 jit_solution(2428440668786410586)
XLA Ops:
  1.3 12.3 %shard_map.113 = (bf16[128,32,256]{2,1,0:T(8,128)(2,1)}, bf16[2,512,512]{2,1,0:T(8,128)(2,1)}, bf16[2,512,512]{2,1,0:T(8,128)(2,1)}) custom-call(s32[1,64]{1,0:T(1,128)} %owner_ref.3, s32[1]{0:T(128)S(6)} %copy.14.count_ref, s32[1]{0:T(128)} %bitcast.me_ref, s32[1,1792]{1,0:T(1,128)} %index.1, f32[1024,1024]{1,0:T(8,128)} %factor.3, f32[1024,256]{1,0:T(8,128)} %rhs.3, ...), custom_call_target="tpu_custom_call" | custom-call | flops 8000000000 | bytes 14000000 | tf_op jit(solution)/shard_map/pallas_call | solution.py:355
  13.6 11.3 %all-to-all-start = ((bf16[128,32,256]{2,1,0:T(8,128)(2,1)}), bf16[128,32,256]{2,1,0:T(8,128)(2,1)S(1)}, u32[]{:S(2)}, u32[]{:S(2)}) async-start(bf16[128,32,256]{2,1,0:T(8,128)(2,1)} %get-tuple-element.15), calls=%async_computation | async-start | bytes 4194304 | tf_op jit(solution)/shard_map/all_to_all | solution.py:415
  24.9 4.3 %shard_map.114 = (bf16[512,512]{1,0:T(8,128)(2,1)S(1)}, bf16[512,512]{1,0:T(8,128)(2,1)S(1)}) custom-call(f32[512,512]{1,0:T(8,128)S(1)} %copy-done.5), custom_call_target="tpu_custom_call" | custom-call | flops 2000000000 | bytes 3000000 | tf_op jit(solution)/shard_map/pallas_call | solution.py:355
  29.3 0.8 copy-done.11
  30.0 0.8 copy-done.13
  30.9 24.3 %all-to-all-done = bf16[128,32,256]{2,1,0:T(8,128)(2,1)S(1)} async-done(((bf16[128,32,256]{2,1,0:T(8,128)(2,1)}), bf16[128,32,256]{2,1,0:T(8,128)(2,1)S(1)}, u32[]{:S(2)}, u32[]{:S(2)}) %all-to-all-start) | async-done | bytes 2097184 | tf_op jit(solution)/shard_map/all_to_all | solution.py:415
  55.1 1.0 copy-done.7
  56.2 1.0 copy-done.12
  57.2 1.0 copy-done.14
  58.2 5.0 %shard_map.115 = (f32[512,256]{1,0:T(8,128)}, bf16[4096,256]{1,0:T(8,128)(2,1)S(1)}) custom-call(bf16[4096,256]{1,0:T(8,128)(2,1)S(1)} %bitcast.10, f32[512,256]{1,0:T(8,128)S(1)} %copy-done.7, bf16[512,512]{1,0:T(8,128)(2,1)S(1)} %copy-done.12, bf16[512,512]{1,0:T(8,128)(2,1)S(1)} %copy-done.14), custom_call_target="tpu_custom_call" | custom-call | flops 3000000000 | bytes 5000000 | tf_op jit(solution)/shard_map/pallas_call | solution.py:355
  63.2 1.3 %copy-done = bf16[4096,256]{1,0:T(8,128)(2,1)} copy-done((bf16[4096,256]{1,0:T(8,128)(2,1)}, bf16[4096,256]{1,0:T(8,128)(2,1)S(1)}, u32[]{:S(2)}) %copy-start) | copy-done | bytes 2097176
  64.6 5.0 %all-to-all-start.1 = ((bf16[128,32,256]{2,1,0:T(8,128)(2,1)}), bf16[128,32,256]{2,1,0:T(8,128)(2,1)S(1)}, u32[]{:S(2)}, u32[]{:S(2)}) async-start(bf16[128,32,256]{2,1,0:T(8,128)(2,1)} %bitcast.9), calls=%async_computation.1 | async-start | bytes 4194304 | tf_op jit(solution)/shard_map/all_to_all | solution.py:415
  69.6 0.1 copy.13.pivot
  69.8 2.2 %copy-done.3 = f32[1024,1024]{1,0:T(8,128)S(1)} copy-done((f32[1024,1024]{1,0:T(8,128)S(1)}, f32[1024,1024]{1,0:T(8,128)}, u32[]{:S(2)}) %copy-start.3) | copy-done | bytes 4194328
  72.0 2.0 %copy-done.4 = bf16[1792,1024]{1,0:T(8,128)(2,1)S(1)} copy-done((bf16[1792,1024]{1,0:T(8,128)(2,1)S(1)}, bf16[1792,1024]{1,0:T(8,128)(2,1)}, u32[]{:S(2)}) %copy-start.4) | copy-done | bytes 3670040
  74.0 1.2 copy-done.6
  75.3 1.2 copy-done.9
  76.5 1.2 copy-done.10
  77.7 7.6 %shard_map.116 = (f32[128,256]{1,0:T(8,128)S(1)}, bf16[128,4096]{1,0:T(8,128)(2,1)S(1)}, bf16[128,4096]{1,0:T(8,128)(2,1)S(1)}) custom-call(s32[1,64]{1,0:T(1,128)S(1)} %copy-done.8, s32[1]{0:T(128)S(6)} %copy.14.count_ref, f32[1024,1024]{1,0:T(8,128)S(1)} %copy-done.3, f32[1024,256]{1,0:T(8,128)S(1)} %copy-done.6, bf16[1792,1024]{1,0:T(8,128)(2,1)S(1)} %copy-done.4, ...), custom_call_target="tpu_custom_call" | custom-call | flops 4000000000 | bytes 11000000 | tf_op jit(solution)/shard_map/pallas_call | solution.py:355
  85.3 1.0 copy-done.1
  86.3 13.5 %all-to-all-done.1 = bf16[128,32,256]{2,1,0:T(8,128)(2,1)S(1)} async-done(((bf16[128,32,256]{2,1,0:T(8,128)(2,1)}), bf16[128,32,256]{2,1,0:T(8,128)(2,1)S(1)}, u32[]{:S(2)}, u32[]{:S(2)}) %all-to-all-start.1) | async-done | bytes 2097184 | tf_op jit(solution)/shard_map/all_to_all | solution.py:415
  99.7 1.2 copy-done.2
  101.0 1.8 %shard_map.117 = (bf16[128,256]{1,0:T(8,128)(2,1)S(1)}, bf16[16,128,256]{2,1,0:T(8,128)(2,1)}) custom-call(f32[128,256]{1,0:T(8,128)S(1)} %get-tuple-element.22.field0, bf16[128,4096]{1,0:T(8,128)(2,1)S(1)} %get-tuple-element.23.g_high, bf16[128,4096]{1,0:T(8,128)(2,1)S(1)} %copy-done.2, bf16[4096,256]{1,0:T(8,128)(2,1)S(1)} %bitcast.7), custom_call_target="tpu_custom_call" | custom-call | flops 600000000 | bytes 5000000 | tf_op jit(solution)/shard_map/pallas_call | solution.py:355
  102.7 3.7 %all-to-all-start.2 = ((bf16[16,128,256]{2,1,0:T(8,128)(2,1)}), bf16[16,128,256]{2,1,0:T(8,128)(2,1)S(1)}, u32[]{:S(2)}, u32[]{:S(2)}) async-start(bf16[16,128,256]{2,1,0:T(8,128)(2,1)} %get-tuple-element.27), calls=%async_computation.2 | async-start | bytes 2097152 | tf_op jit(solution)/shard_map/all_to_all | solution.py:487
  106.5 1.2 collective-permute-done
  107.8 0.6 collective-permute-start.3
  108.4 2.1 %collective-permute-start.2 = (bf16[2,128,256]{2,1,0:T(8,128)(2,1)S(1)}, bf16[2,128,256]{2,1,0:T(8,128)(2,1)S(1)}, u32[]{:S(2)}, u32[]{:S(2)}) collective-permute-start(bf16[2,128,256]{2,1,0:T(8,128)(2,1)S(1)} %pad_maximum_fusion.pair), channel_id=1, source_target_pairs={{0,4},{1,5},{2,6},{3,7},{4,0},{5,1},{6,2},{7,3},{8,12},{9,13},{10,... | collective-permute-start | bytes 393224 | tf_op jit(solution)/shard_map/ppermute | solution.py:493
  110.5 1.4 %collective-permute-start.1 = (bf16[2,128,256]{2,1,0:T(8,128)(2,1)S(1)}, bf16[2,128,256]{2,1,0:T(8,128)(2,1)S(1)}, u32[]{:S(2)}, u32[]{:S(2)}) collective-permute-start(bf16[2,128,256]{2,1,0:T(8,128)(2,1)S(1)} %pad_maximum_fusion.pair), channel_id=1, source_target_pairs={{0,2},{1,3},{2,0},{3,1},{4,6},{5,7},{6,4},{7,5},{8,10},{9,11},{10,... | collective-permute-start | bytes 393224 | tf_op jit(solution)/shard_map/ppermute | solution.py:493
  111.9 5.5 %collective-permute-done.3.refs_2_ = bf16[2,128,256]{2,1,0:T(8,128)(2,1)S(1)} collective-permute-done((bf16[2,128,256]{2,1,0:T(8,128)(2,1)S(1)}, bf16[2,128,256]{2,1,0:T(8,128)(2,1)S(1)}, u32[]{:S(2)}, u32[]{:S(2)}) %collective-permute-start.3) | collective-permute-done | bytes 131104 | tf_op jit(solution)/shard_map/ppermute | solution.py:493
  117.4 0.6 collective-permute-done.1.refs_0_
  118.0 6.0 %all-to-all-done.2 = bf16[16,128,256]{2,1,0:T(8,128)(2,1)S(1)} async-done(((bf16[16,128,256]{2,1,0:T(8,128)(2,1)}), bf16[16,128,256]{2,1,0:T(8,128)(2,1)S(1)}, u32[]{:S(2)}, u32[]{:S(2)}) %all-to-all-start.2) | async-done | bytes 1048608 | tf_op jit(solution)/shard_map/all_to_all | solution.py:487
  124.0 4.3 %shard_map.118 = f32[1024,2048]{1,0:T(8,128)} custom-call(s32[1]{0:T(128)} %bitcast.me_ref, bf16[2,128,256]{2,1,0:T(8,128)(2,1)S(1)} %pad_maximum_fusion.pair, bf16[2,128,256]{2,1,0:T(8,128)(2,1)S(1)} %collective-permute-done.1.refs_0_, bf16[2,128,256]{2,1,0:T(8,128)(2,1)S(1)} %collective-permute-done.2.refs_1_, ...), custom_call_target="tpu_custom_call" | custom-call | flops 1000000000 | bytes 10000000 | tf_op jit(solution)/shard_map/pallas_call | solution.py:355
  (25 shorter events, 0.2 us)
Async XLA Ops:
  13.6 11.3 %copy-start.5 = (f32[512,512]{1,0:T(8,128)S(1)}, f32[512,512]{1,0:T(8,128)}, u32[]{:S(2)}) copy-start(f32[512,512]{1,0:T(8,128)} %sep_hbm.1) | copy-start | bytes 3145732
  13.6 41.5 %all-to-all-start = ((bf16[128,32,256]{2,1,0:T(8,128)(2,1)}), bf16[128,32,256]{2,1,0:T(8,128)(2,1)S(1)}, u32[]{:S(2)}, u32[]{:S(2)}) async-start(bf16[128,32,256]{2,1,0:T(8,128)(2,1)} %get-tuple-element.15), calls=%async_computation | async-start | bytes 4194304 | tf_op jit(solution)/shard_map/all_to_all | solution.py:415
  29.2 0.8 copy-start.11
  30.0 0.8 copy-start.13
  55.1 1.0 copy-start.7
  56.2 1.0 copy-start.12
  57.2 1.0 copy-start.14
  63.2 1.3 %copy-start = (bf16[4096,256]{1,0:T(8,128)(2,1)}, bf16[4096,256]{1,0:T(8,128)(2,1)S(1)}, u32[]{:S(2)}) copy-start(bf16[4096,256]{1,0:T(8,128)(2,1)S(1)} %get-tuple-element.25) | copy-start | bytes 6291460
  64.6 5.0 %copy-start.15 = (s32[128,8]{0,1:T(8,128)S(1)}, s32[128,8]{0,1:T(8,128)}, u32[]{:S(2)}) copy-start(s32[128,8]{0,1:T(8,128)} %param.19) | copy-start | bytes 12292
  64.6 5.1 %copy-start.16 = (f32[128,8]{0,1:T(8,128)S(1)}, f32[128,8]{0,1:T(8,128)}, u32[]{:S(2)}) copy-start(f32[128,8]{0,1:T(8,128)} %param.18) | copy-start | bytes 12292
  64.6 5.2 %copy-start.8 = (s32[1,64]{1,0:T(1,128)S(1)}, s32[1,64]{1,0:T(1,128)}, u32[]{:S(2)}) copy-start(s32[1,64]{1,0:T(1,128)} %owner_ref.3) | copy-start | bytes 772
  64.6 35.2 %all-to-all-start.1 = ((bf16[128,32,256]{2,1,0:T(8,128)(2,1)}), bf16[128,32,256]{2,1,0:T(8,128)(2,1)S(1)}, u32[]{:S(2)}, u32[]{:S(2)}) async-start(bf16[128,32,256]{2,1,0:T(8,128)(2,1)} %bitcast.9), calls=%async_computation.1 | async-start | bytes 4194304 | tf_op jit(solution)/shard_map/all_to_all | solution.py:415
  69.8 2.2 %copy-start.3 = (f32[1024,1024]{1,0:T(8,128)S(1)}, f32[1024,1024]{1,0:T(8,128)}, u32[]{:S(2)}) copy-start(f32[1024,1024]{1,0:T(8,128)} %factor.3) | copy-start | bytes 12582916
  72.0 2.0 %copy-start.4 = (bf16[1792,1024]{1,0:T(8,128)(2,1)S(1)}, bf16[1792,1024]{1,0:T(8,128)(2,1)}, u32[]{:S(2)}) copy-start(bf16[1792,1024]{1,0:T(8,128)(2,1)} %coupling.3) | copy-start | bytes 11010052
  74.0 1.2 copy-start.6
  75.2 1.2 copy-start.9
  76.5 1.2 copy-start.10
  85.3 1.0 copy-start.1
  99.7 1.2 copy-start.2
  102.7 21.3 %all-to-all-start.2 = ((bf16[16,128,256]{2,1,0:T(8,128)(2,1)}), bf16[16,128,256]{2,1,0:T(8,128)(2,1)S(1)}, u32[]{:S(2)}, u32[]{:S(2)}) async-start(bf16[16,128,256]{2,1,0:T(8,128)(2,1)} %get-tuple-element.27), calls=%async_computation.2 | async-start | bytes 2097152 | tf_op jit(solution)/shard_map/all_to_all | solution.py:487
  106.4 1.3 %collective-permute-start = (bf16[128,256]{1,0:T(8,128)(2,1)S(1)}, bf16[128,256]{1,0:T(8,128)(2,1)S(1)}, u32[]{:S(2)}, u32[]{:S(2)}) collective-permute-start(bf16[128,256]{1,0:T(8,128)(2,1)S(1)} %get-tuple-element.26), channel_id=1, source_target_pairs={{0,1},{1,0},{2,3},{3,2},{4,5},{5,4},{6,7},{7,6},{8,9},{9,8},{10,11... | collective-permute-start | bytes 196616 | tf_op jit(solution)/shard_map/ppermute | solution.py:490
  107.8 9.7 %collective-permute-start.3 = (bf16[2,128,256]{2,1,0:T(8,128)(2,1)S(1)}, bf16[2,128,256]{2,1,0:T(8,128)(2,1)S(1)}, u32[]{:S(2)}, u32[]{:S(2)}) collective-permute-start(bf16[2,128,256]{2,1,0:T(8,128)(2,1)S(1)} %pad_maximum_fusion.pair), channel_id=1, source_target_pairs={{0,6},{1,7},{2,4},{3,5},{4,2},{5,3},{6,0},{7,1},{8,14},{9,15},{10,... | collective-permute-start | bytes 393224 | tf_op jit(solution)/shard_map/ppermute | solution.py:493
  108.4 9.0 %collective-permute-start.2 = (bf16[2,128,256]{2,1,0:T(8,128)(2,1)S(1)}, bf16[2,128,256]{2,1,0:T(8,128)(2,1)S(1)}, u32[]{:S(2)}, u32[]{:S(2)}) collective-permute-start(bf16[2,128,256]{2,1,0:T(8,128)(2,1)S(1)} %pad_maximum_fusion.pair), channel_id=1, source_target_pairs={{0,4},{1,5},{2,6},{3,7},{4,0},{5,1},{6,2},{7,3},{8,12},{9,13},{10,... | collective-permute-start | bytes 393224 | tf_op jit(solution)/shard_map/ppermute | solution.py:493
  110.5 7.5 %collective-permute-start.1 = (bf16[2,128,256]{2,1,0:T(8,128)(2,1)S(1)}, bf16[2,128,256]{2,1,0:T(8,128)(2,1)S(1)}, u32[]{:S(2)}, u32[]{:S(2)}) collective-permute-start(bf16[2,128,256]{2,1,0:T(8,128)(2,1)S(1)} %pad_maximum_fusion.pair), channel_id=1, source_target_pairs={{0,2},{1,3},{2,0},{3,1},{4,6},{5,7},{6,4},{7,5},{8,10},{9,11},{10,... | collective-permute-start | bytes 393224 | tf_op jit(solution)/shard_map/ppermute | solution.py:493

commit v3 on v2

--- a/solution.py
+++ b/solution.py
@@ -12,6 +12,7 @@
 UNIT = 128
 BASE = 256
 WIDE = 512
+FULL = 60.5
 PAD = 32
 LANES = 128
 VMEM = pltpu.VMEM
@@ -47,7 +48,7 @@
     return mm3(a, (on_diagonal(b[0]), on_diagonal(b[1])))
 
 
-def invert_lower(read, count):
+def invert_lower(read, count, midway=None):
     row = lax.broadcasted_iota(jnp.int32, (UNIT, 2 * UNIT), 0)
     col = lax.broadcasted_iota(jnp.int32, (UNIT, 2 * UNIT), 1) & (UNIT - 1)
     first = lax.broadcasted_iota(jnp.int32, (UNIT, 2 * UNIT), 1) < UNIT
@@ -72,6 +73,8 @@
         found.append(jnp.where(row == col, down, below_it))
     level = 1
     while (1 << level) < UNIT:
+        if level == 3 and midway is not None:
+            midway()
         mask = below(level)
         parts = [split(one) for one in found]
         halves = [mm_pair(p, split(jnp.where(mask, pair, 0.0))) for p, pair in zip(parts, pairs)]
@@ -95,6 +98,33 @@
     return result
 
 
+def solve_rows(rows, high, low, off):
+    half = off[0].shape[0]
+    inv = [(high[i], low[i]) for i in range(2)]
+    x0 = mm3(split(rows[:, :half]), inv[0], NT)
+    x1 = mm3(split(rows[:, half:] - mm3(split(x0), off, NT)), inv[1], NT)
+    y1 = mm3(split(x1), inv[1])
+    y0 = mm3(split(x0 - mm3(split(y1), off)), inv[0])
+    return y0, y1
+
+
+def copy_all(pairs, sems, first=0):
+    return [
+        pltpu.make_async_copy(source, target, sems.at[first + k])
+        for k, (source, target) in enumerate(pairs)
+    ]
+
+
+def start(copies):
+    for copy in copies:
+        copy.start()
+
+
+def wait(copies):
+    for copy in copies:
+        copy.wait()
+
+
 def place_rows(source, target, owner_ref, count, slots, halves, extra=None):
     width = target.shape[2]
     row = lax.broadcasted_iota(jnp.int32, (PAD, width), 0)
@@ -118,21 +148,26 @@
 def forward_kernel(
     owner_ref, count_ref, me_ref, index, factor, rhs, coupling,
     out_hbm, high_out, low_out,
-    diag, lower, right, block, high, low, contrib, out, sems,
+    diag, between, lower, right, block, high, low, contrib, out, sems,
 ):
-    half = diag.shape[1]
+    quarters = diag.shape[0]
+    half = lower.shape[0]
     bound = coupling.shape[0]
     halves = owner_ref.shape[1]
     slots = bound // halves
-    copies = [
-        pltpu.make_async_copy(factor.at[0:half, 0:half], diag.at[0], sems.at[0]),
-        pltpu.make_async_copy(factor.at[half : 2 * half, half : 2 * half], diag.at[1], sems.at[1]),
-        pltpu.make_async_copy(rhs, right, sems.at[2]),
-        pltpu.make_async_copy(factor.at[half : 2 * half, 0:half], lower, sems.at[3]),
-        pltpu.make_async_copy(coupling, block, sems.at[4]),
-    ]
-    for copy in copies:
-        copy.start()
+    pieces = 4
+
+    def tile(i, k):
+        return factor.at[i * BASE : (i + 1) * BASE, k * BASE : (k + 1) * BASE]
+
+    factor_copies = copy_all([(tile(k, k), diag.at[k]) for k in range(quarters)], sems)
+    rest_copies = copy_all(
+        [(tile(2 * i + 1, 2 * i), between.at[i]) for i in range(2)]
+        + [(rhs, right), (factor.at[half : 2 * half, 0:half], lower), (coupling, block)],
+        sems,
+        quarters,
+    )
+    start(factor_copies + rest_copies)
     out[...] = jnp.zeros_like(out)
     contrib[bound:, :] = jnp.zeros((contrib.shape[0] - bound, contrib.shape[1]), F32)
     mine = group_of(lax.broadcasted_iota(jnp.int32, (halves, bound), 1)) == (
@@ -146,55 +181,53 @@
     part = me_ref[0] & (LANES // PAD - 1)
     fold = one_hot((at - slots * group_of(at)) + PAD * part == lane)
     extra = side_by_side(mm(low_bits, fold), mm(high_bits, fold))
-    copies[0].wait()
-    copies[1].wait()
+    wait(factor_copies)
 
     def read(b, i, k):
-        top = (b % 2) * BASE
-        return diag[
-            b // 2, top + i * UNIT : top + (i + 1) * UNIT, top + k * UNIT : top + (k + 1) * UNIT
-        ]
-
-    inverses = invert_lower(read, 4)
+        return diag[b, i * UNIT : (i + 1) * UNIT, k * UNIT : (k + 1) * UNIT]
+
+    sides = []
+
+    def midway():
+        wait(rest_copies[:4])
+        sides.extend((right[...].T, split(lower[...])))
+
+    inverses = invert_lower(read, quarters, midway)
     for i in range(2):
         first_parts, second_parts = split(inverses[2 * i]), split(inverses[2 * i + 1])
-        between = split(diag[i, BASE:, :BASE])
-        corner = split(-mm3(second_parts, split(mm3(between, first_parts))))
+        corner = split(-mm3(second_parts, split(mm3(split(between[i]), first_parts))))
         for k, ref in enumerate((high, low)):
             ref[i, :BASE, :BASE] = first_parts[k]
             ref[i, BASE:, BASE:] = second_parts[k]
             ref[i, BASE:, :BASE] = corner[k]
             ref[i, :BASE, BASE:] = jnp.zeros((BASE, BASE), BF16)
-    keep = [
-        pltpu.make_async_copy(high, high_out, sems.at[5]),
-        pltpu.make_async_copy(low, low_out, sems.at[6]),
-    ]
-    for copy in keep:
-        copy.start()
-    copies[2].wait()
-    copies[3].wait()
-    inv = [(high[i], low[i]) for i in range(2)]
-    off = split(lower[...])
-    turned = right[...].T
-    x0 = mm3(split(turned[:, :half]), inv[0], NT)
-    x1 = mm3(split(turned[:, half:] - mm3(split(x0), off, NT)), inv[1], NT)
-    y1 = mm3(split(x1), inv[1])
-    y0 = mm3(split(x0 - mm3(split(y1), off)), inv[0])
-    copies[4].wait()
+    keep = copy_all([(high, high_out), (low, low_out)], sems)
+    start(keep)
+    y0, y1 = solve_rows(sides[0], high, low, sides[1])
+    wait(rest_copies[4:])
     contrib[:bound, :] = mm(block[:, :half], y0.astype(BF16), NT) + mm(
         block[:, half:], y1.astype(BF16), NT
     )
     place_rows(contrib, out, owner_ref, count_ref[0], slots, halves, extra)
-    keep.append(pltpu.make_async_copy(out, out_hbm, sems.at[0]))
-    keep[-1].start()
-    for copy in keep:
-        copy.wait()
-
-
-def schur_kernel(sep_hbm, s_high, s_low, sep, sem):
-    copy = pltpu.make_async_copy(sep_hbm, sep, sem)
-    copy.start()
-    copy.wait()
+    size = out.shape[0] // pieces
+    send = copy_all(
+        [
+            (out.at[k * size : (k + 1) * size], out_hbm.at[k * size : (k + 1) * size])
+            for k in range(pieces)
+        ],
+        sems,
+        quarters,
+    )
+    start(send)
+    wait(keep)
+    wait(send)
+
+
+def schur_kernel(sep_hbm, rhs_hbm, both, sep, sems):
+    order = sep.shape[0]
+    copies = copy_all([(sep_hbm, sep), (rhs_hbm, both.at[:, order:])], sems)
+    start(copies)
+    copies[0].wait()
 
     def read(b, i, k):
         top = b * BASE
@@ -213,7 +246,8 @@
     )
     for i, k, piece in pieces:
         at = (slice(i * BASE, (i + 1) * BASE), slice(k * BASE, (k + 1) * BASE))
-        s_high[at], s_low[at] = split(piece)
+        both[at] = piece
+    copies[1].wait()
 
 
 def project_kernel(
@@ -241,12 +275,7 @@
         project += jnp.where(places == pivot[:, k : k + 1], weight[:, k : k + 1], 0.0)
     for copy in copies[:3]:
         copy.wait()
-    inv = [(high[i], low[i]) for i in range(2)]
-    off = split(lower[...])
-    x0 = mm3(split(project[:, :half]), inv[0], NT)
-    x1 = mm3(split(project[:, half:] - mm3(split(x0), off, NT)), inv[1], NT)
-    y1 = mm3(split(x1), inv[1])
-    y0 = mm3(split(x0 - mm3(split(y1), off)), inv[0])
+    y0, y1 = solve_rows(project, high, low, split(lower[...]))
     y0, y1 = split(y0), split(y1)
     copies[3].wait()
     field0[...] = mm3(y0, split(right[:half, :])) + mm3(y1, split(right[half:, :]))
@@ -268,16 +297,15 @@
 
 
 def separator_kernel(
-    incoming, rhs_hbm, high_hbm, low_hbm, potential, replies, right, high, low, sems, *, fronts, slots
+    incoming, schur_hbm, potential_hbm, replies_hbm, schur, potential, replies, sems, *, slots
 ):
-    copies = [
-        pltpu.make_async_copy(source, target, sems.at[k])
-        for k, (source, target) in enumerate(((rhs_hbm, right), (high_hbm, high), (low_hbm, low)))
-    ]
-    for copy in copies:
-        copy.start()
+    fronts = incoming.shape[0]
+    chunks = fronts * PAD // WIDE
+    per = WIDE // PAD
+    rest = copy_all([(schur_hbm, schur)], sems)
+    start(rest)
     group = LANES // PAD
-    tail = incoming[...].reshape(fronts, PAD, -1)[:, PAD - 8 :, :].astype(F32)
+    tail = incoming[:, PAD - 8 :, :].astype(F32)
     tail = tail.reshape(fronts // group, group, 8, -1)
     tail = (tail[:, 0] + tail[:, 1]) + (tail[:, 2] + tail[:, 3])
     tail = tail[:, slots - (PAD - 8), :]
@@ -285,27 +313,29 @@
     rows = [jnp.where(high_bits == 1.0 + p, low_bits, -1.0) for p in range(2)]
     empty = jnp.full((LANES - rows[0].shape[0], LANES), -1.0, F32)
     cols = [jnp.concatenate([one, empty], axis=0).T for one in rows]
-    part = right.shape[0] // 2
+    order = schur.shape[0]
+    part = order // 2
     down = lax.broadcasted_iota(jnp.int32, (part, LANES), 0).astype(F32).astype(BF16)
     along = lax.broadcasted_iota(jnp.int32, (LANES, part), 1).astype(F32).astype(BF16)
-    groups = incoming.shape[0] // LANES
     each = WIDE // LANES
     total = None
-    for c in range(groups // each):
+    for c in range(chunks):
         tiles = [
             jnp.concatenate(
                 [pick(down == rows[p][g : g + 1, :].astype(BF16)) for p in range(2)], axis=0
             )
             for g in range(c * each, (c + 1) * each)
         ]
-        term = mm(jnp.concatenate(tiles, axis=1), incoming[c * WIDE : (c + 1) * WIDE, :])
+        values = incoming[c * per : (c + 1) * per].reshape(WIDE, -1)
+        term = mm(jnp.concatenate(tiles, axis=1), values)
         total = term if total is None else total + term
-    for copy in copies:
-        copy.wait()
-    found = mm3((high[...], low[...]), split(right[...] - total))
+    wait(rest)
+    found = mm3(split(schur[:, :order]), split(schur[:, order:] - total))
     potential[...] = found
+    stores = copy_all([(potential, potential_hbm)], sems)
+    start(stores)
     rounded = found.astype(BF16)
-    for c in range(groups // each):
+    for c in range(chunks):
         tiles = [
             jnp.concatenate(
                 [pick(along == cols[p][:, g : g + 1].astype(BF16)) for p in range(2)], axis=1
@@ -313,7 +343,15 @@
             for g in range(c * each, (c + 1) * each)
         ]
         chosen = jnp.concatenate(tiles, axis=0)
-        replies[c * WIDE : (c + 1) * WIDE, :] = mm(chosen, rounded).astype(BF16)
+        replies[c * per : (c + 1) * per] = (
+            mm(chosen, rounded).astype(BF16).reshape(per, PAD, rounded.shape[1])
+        )
+        if (c + 1) % (chunks // 2) == 0:
+            first = (c + 1 - chunks // 2) * per
+            last = (c + 1) * per
+            stores += copy_all([(replies.at[first:last], replies_hbm.at[first:last])], sems, 1 + c)
+            stores[-1].start()
+    wait(stores)
 
 
 def field_kernel(field0, g_high, g_low, returned, field, spread):
@@ -329,26 +367,23 @@
     row_tile, tiles, sems = refs[-3:]
     scale = 1.0 / col_tile.shape[1]
     me = me_ref[0]
+    slots, height, _ = tiles.shape
     for d, block in enumerate((pair,) + others):
-        row_tile[me ^ (2 * d)] = block[0]
-        row_tile[me ^ (2 * d + 1)] = block[1]
+        for k in range(2):
+            row_tile[me ^ (2 * d + k)] = block[k]
     rows = row_tile[...].reshape(-1, col_tile.shape[1])
-    slots, _, width = tiles.shape
+    columns = col_tile[...]
     copies = []
-    for t in range(hess.shape[1] // width):
+    for t in range(hess.shape[0] // height):
         slot = t % slots
         if t >= slots:
             copies[t - slots].wait()
-        gram = mm(rows, col_tile[t * width : (t + 1) * width, :], NT) * scale
+        at = slice(t * height, (t + 1) * height)
+        gram = mm(rows[at, :], columns, NT) * scale
         tiles[slot] = gram * gram
-        copies.append(
-            pltpu.make_async_copy(
-                tiles.at[slot], hess.at[:, t * width : (t + 1) * width], sems.at[slot]
-            )
-        )
+        copies += copy_all([(tiles.at[slot], hess.at[at])], sems, slot)
         copies[-1].start()
-    for copy in copies[-slots:]:
-        copy.wait()
+    wait(copies[-slots:])
 
 
 def call(kernel, outs, ins, scratch, specs, out_specs, flops, moved, vmem):
@@ -358,7 +393,7 @@
         in_specs=specs,
         out_specs=out_specs,
         scratch_shapes=scratch,
-        compiler_params=pltpu.CompilerParams(vmem_limit_bytes=vmem * 1024 * 1024),
+        compiler_params=pltpu.CompilerParams(vmem_limit_bytes=int(vmem * 1024 * 1024)),
         cost_estimate=pl.CostEstimate(flops=flops, bytes_accessed=moved, transcendentals=0),
     )(*ins)
 
@@ -394,7 +429,8 @@
         ),
         (sep_owner, bound_count, me, sep_index, front_factor, rhs, coupling),
         [
-            VMEM((2, half, half), F32),
+            VMEM((order // BASE, BASE, BASE), F32),
+            VMEM((2, BASE, BASE), F32),
             VMEM((half, half), F32),
             VMEM((order, sources), F32),
             VMEM((bound, order), BF16),
@@ -402,7 +438,7 @@
             VMEM((2, half, half), BF16),
             VMEM((bound + 8, sources), F32),
             VMEM((fronts, PAD, sources), BF16),
-            dma((7,)),
+            dma((9,)),
         ],
         [sm, sm, sm, vm, hbm, hbm, hbm],
         (hbm,) * 3,
@@ -413,39 +449,21 @@
 
     def exchange(blocks):
         return lax.all_to_all(
-            blocks.reshape(fronts, PAD, sources), both, split_axis=0, concat_axis=0, tiled=True
-        ).reshape(flat, sources)
+            blocks, both, split_axis=0, concat_axis=0, tiled=True
+        )
 
     incoming = exchange(outgoing)
-    s_high, s_low = call(
+    schur = call(
         schur_kernel,
-        (shape((sep_size, sep_size), BF16), shape((sep_size, sep_size), BF16)),
-        (sep_factor,),
-        [VMEM((sep_size, sep_size), F32), dma],
-        [hbm],
-        (vm, vm),
+        shape((sep_size, sep_size + sources), F32),
+        (sep_factor, sep_rhs),
+        [VMEM((sep_size, sep_size), F32), dma((2,))],
+        [hbm, hbm],
+        vm,
         2_000_000_000,
         3_000_000,
         24,
     )
-    sep_potential, replies = call(
-        lambda *refs: separator_kernel(*refs, fronts=fronts, slots=bound // halves),
-        (shape((sep_size, sources), F32), shape((flat, sources), BF16)),
-        (incoming, sep_rhs, s_high, s_low),
-        [
-            VMEM((sep_size, sources), F32),
-            VMEM((sep_size, sep_size), BF16),
-            VMEM((sep_size, sep_size), BF16),
-            dma((3,)),
-        ],
-        [vm, hbm, hbm, hbm],
-        (vm, vm),
-        3_000_000_000,
-        5_000_000,
-        28,
-    )
-    returned = exchange(replies)
-    weight, _ = lax.optimization_barrier((cell_weight, sep_potential))
     field0, g_high, g_low = call(
         project_kernel,
         (
@@ -455,7 +473,7 @@
         ),
         (
             sep_owner, bound_count, front_factor, rhs, coupling, inv_high, inv_low,
-            weight, cell_pivot,
+            cell_weight, cell_pivot,
         ),
         [
             VMEM((half, half), F32),
@@ -471,8 +489,26 @@
         (vm,) * 3,
         4_000_000_000,
         11_000_000,
-        32,
-    )
+        36,
+    )
+    schur, _ = lax.optimization_barrier((schur, g_high))
+    sep_potential, replies = call(
+        lambda *refs: separator_kernel(*refs, slots=bound // halves),
+        (shape((sep_size, sources), F32), shape((fronts, PAD, sources), BF16)),
+        (incoming, schur),
+        [
+            VMEM((sep_size, sep_size + sources), F32),
+            VMEM((sep_size, sources), F32),
+            VMEM((fronts, PAD, sources), BF16),
+            dma((flat // WIDE + 1,)),
+        ],
+        [vm, hbm],
+        (hbm, hbm),
+        3_000_000_000,
+        5_000_000,
+        FULL,
+    )
+    returned = exchange(replies).reshape(flat, sources)
     field, spread = call(
         field_kernel,
         (shape((cells, sources), BF16), shape((row_count, cells, sources), BF16)),
@@ -499,7 +535,7 @@
         (me, pair, *others, col_tile),
         [
             VMEM((col_count, cells, sources), BF16),
-            VMEM((4, col_count * cells, BASE), F32),
+            VMEM((4, BASE, row_count * cells), F32),
             dma((4,)),
         ],
         [sm] + [vm] * (col_count // 2 + 1),

time: 129 us -> 125 us (0.969)
  blocking collectives: 0 us -> 35.5 us
  waiting for transfers between devices: 51.1 us -> 27.7 us
  local copies, waits for them, and re-layouts: 16.4 us -> 3.43 us
  starting transfers between devices: 24.2 us -> 19.8 us
  Pallas kernels: 35.2 us -> 36.9 us
    all_to_all x0 -> x1, blocking collectives: none -> 35.5 us  [exchange(): return lax.all_to_all(blocks, both, split_axis=0, concat_axis=0, tiled=True)]
    all_to_all x2 -> x1, waiting for transfers between devices: 37.7 us -> 14.3 us  [exchange(): return lax.all_to_all(blocks, both, split_axis=0, concat_axis=0, tiled=True)]
    unnamed x35 -> x24, local copies, waits for them, and re-layouts: 16.2 us -> 3.43 us
    all_to_all x2 -> x1, starting transfers between devices: 16.3 us -> 11.9 us  [exchange(): return lax.all_to_all(blocks, both, split_axis=0, concat_axis=0, tiled=True)]
    pallas_call x6, Pallas kernels: 35.2 us -> 36.9 us  [call(): pl.pallas_call(kernel, out_shape=outs, in_specs=specs, out_specs=out_spec...]
  transfers between devices with their start and end apart: 7 -> 6, of which waited for: 6 -> 5; matrix products, arithmetic and copies ran while one was open for 0% -> 0% of each run, Pallas kernels for 9% -> 10%
where the time goes in v3:
time: 125 us
  Pallas kernels  36.9 us (30%)
  blocking collectives  35.5 us (28%)
  waiting for transfers between devices  27.7 us (22%)
  starting transfers between devices  19.8 us (16%)
  local copies, waits for them, and re-layouts  3.43 us (3%)
  between operations  1.64 us (1%)
    pallas_call x6, Pallas kernels, call(): pl.pallas_call(kernel, out_shape=outs, in_specs=specs, out_specs=out_spec...  36.9 us
    all_to_all x1, blocking collectives, exchange(): return lax.all_to_all(blocks, both, split_axis=0, concat_axis=0, tiled=True)  35.5 us
    all_to_all x1, waiting for transfers between devices, exchange(): return lax.all_to_all(blocks, both, split_axis=0, concat_axis=0, tiled=True)  14.3 us
    all_to_all x1, starting transfers between devices, exchange(): return lax.all_to_all(blocks, both, split_axis=0, concat_axis=0, tiled=True)  11.9 us
    ppermute x3, waiting for transfers between devices, local(): lax.ppermute(pair, 'col', [(i, i ^ 2 * d) for i in range(col_count)])  6.1 us
    all_to_all x1, waiting for transfers between devices, local(): lax.all_to_all(spread, 'row', split_axis=0, concat_axis=0, tiled=True)  6 us
    ppermute x3, starting transfers between devices, local(): lax.ppermute(pair, 'col', [(i, i ^ 2 * d) for i in range(col_count)])  4.17 us
    all_to_all x1, starting transfers between devices, local(): lax.all_to_all(spread, 'row', split_axis=0, concat_axis=0, tiled=True)  3.66 us
  transfers between devices with their start and end apart: 6, of which 5 were waited for; matrix products, arithmetic and copies ran while one was open for 0% of the time, Pallas kernels for 10%

profile of v3, /device:TPU:0, one launch (start us, length us, event | category | flops | bytes accessed | tf_op | source)
XLA Modules:
  0.0 124.9 jit_solution(3913042925073750915)
XLA Ops:
  1.3 11.9 %shard_map.113 = (bf16[128,32,256]{2,1,0:T(8,128)(2,1)}, bf16[2,512,512]{2,1,0:T(8,128)(2,1)}, bf16[2,512,512]{2,1,0:T(8,128)(2,1)}) custom-call(s32[1,64]{1,0:T(1,128)} %owner_ref.3, s32[1]{0:T(128)S(6)} %copy.14.count_ref, s32[1]{0:T(128)} %bitcast.me_ref, s32[1,1792]{1,0:T(1,128)} %index.1, f32[1024,1024]{1,0:T(8,128)} %factor.3, f32[1024,256]{1,0:T(8,128)} %rhs.3, ...), custom_call_target="tpu_custom_call" | custom-call | flops 8000000000 | bytes 14000000 | tf_op jit(solution)/shard_map/pallas_call | solution.py:390
  13.2 0.0 copy-start.9
  13.2 0.0 copy-start.10
  13.2 0.0 copy-start.2
  13.2 0.0 copy-start.4
  13.2 11.9 %all-to-all-start = ((bf16[128,32,256]{2,1,0:T(8,128)(2,1)}), bf16[128,32,256]{2,1,0:T(8,128)(2,1)}, u32[]{:S(2)}, u32[]{:S(2)}) async-start(bf16[128,32,256]{2,1,0:T(8,128)(2,1)} %get-tuple-element.13), calls=%async_computation | async-start | bytes 4194304 | tf_op jit(solution)/shard_map/all_to_all | solution.py:451
  25.1 0.1 copy.12.weight
  25.2 0.0 copy-done.10
  25.2 0.1 copy.13.pivot
  25.3 0.0 copy-start
  25.3 0.0 copy-start.3
  25.3 0.0 copy-start.5
  25.4 4.4 %shard_map.114.refs_1_ = f32[512,768]{1,0:T(8,128)S(1)} custom-call(f32[512,512]{1,0:T(8,128)S(1)} %copy-done.2, f32[512,256]{1,0:T(8,128)S(1)} %copy-done.4), custom_call_target="tpu_custom_call" | custom-call | flops 2000000000 | bytes 3000000 | tf_op jit(solution)/shard_map/pallas_call | solution.py:390
  29.8 1.1 copy-done.6
  30.9 0.0 copy-start.1
  30.9 2.0 %copy-done.1 = bf16[1792,1024]{1,0:T(8,128)(2,1)S(1)} copy-done((bf16[1792,1024]{1,0:T(8,128)(2,1)S(1)}, bf16[1792,1024]{1,0:T(8,128)(2,1)}, u32[]{:S(2)}) %copy-start.1) | copy-done | bytes 3670040
  33.0 7.6 %shard_map.115 = (f32[128,256]{1,0:T(8,128)S(1)}, bf16[128,4096]{1,0:T(8,128)(2,1)S(1)}, bf16[128,4096]{1,0:T(8,128)(2,1)S(1)}) custom-call(s32[1,64]{1,0:T(1,128)S(1)} %copy-done.5, s32[1]{0:T(128)S(6)} %copy.14.count_ref, f32[1024,1024]{1,0:T(8,128)S(1)} %copy-done, f32[1024,256]{1,0:T(8,128)S(1)} %copy-done.3, bf16[1792,1024]{1,0:T(8,128)(2,1)S(1)} %copy-done.1, ...), custom_call_target="tpu_custom_call" | custom-call | flops 4000000000 | bytes 11000000 | tf_op jit(solution)/shard_map/pallas_call | solution.py:390
  40.5 14.3 %all-to-all-done.refs_0_ = bf16[128,32,256]{2,1,0:T(8,128)(2,1)} async-done(((bf16[128,32,256]{2,1,0:T(8,128)(2,1)}), bf16[128,32,256]{2,1,0:T(8,128)(2,1)}, u32[]{:S(2)}, u32[]{:S(2)}) %all-to-all-start) | async-done | bytes 2097184 | tf_op jit(solution)/shard_map/all_to_all | solution.py:451
  54.9 7.5 %shard_map.116 = (f32[512,256]{1,0:T(8,128)}, bf16[128,32,256]{2,1,0:T(8,128)(2,1)}) custom-call(bf16[128,32,256]{2,1,0:T(8,128)(2,1)} %all-to-all-done.refs_0_, f32[512,768]{1,0:T(8,128)} %copy-done.6), custom_call_target="tpu_custom_call" | custom-call | flops 3000000000 | bytes 5000000 | tf_op jit(solution)/shard_map/pallas_call | solution.py:390
  62.4 35.5 %all_to_all.15 = bf16[128,32,256]{2,1,0:T(8,128)(2,1)S(1)} all-to-all(bf16[128,32,256]{2,1,0:T(8,128)(2,1)} %get-tuple-element.21), channel_id=1, replica_groups=mesh['row'=16,'col'=8] {'row','col'}, dimensions={0} | all-to-all | bytes 4194304 | tf_op jit(solution)/shard_map/all_to_all | solution.py:451
  97.9 1.8 %shard_map.117 = (bf16[128,256]{1,0:T(8,128)(2,1)S(1)}, bf16[16,128,256]{2,1,0:T(8,128)(2,1)}) custom-call(f32[128,256]{1,0:T(8,128)S(1)} %get-tuple-element.19.field0, bf16[128,4096]{1,0:T(8,128)(2,1)S(1)} %get-tuple-element.16.g_high, bf16[128,4096]{1,0:T(8,128)(2,1)S(1)} %get-tuple-element.20.g_low, bf16[4096,256]{1,0:T(8,128)(2,1)S(1)} %bitcast.5), custom_call_target="tpu_custom_call" | custom-call | flops 600000000 | bytes 5000000 | tf_op jit(solution)/shard_map/pallas_call | solution.py:390
  99.6 3.7 %all-to-all-start.2 = ((bf16[16,128,256]{2,1,0:T(8,128)(2,1)}), bf16[16,128,256]{2,1,0:T(8,128)(2,1)S(1)}, u32[]{:S(2)}, u32[]{:S(2)}) async-start(bf16[16,128,256]{2,1,0:T(8,128)(2,1)} %get-tuple-element.23), calls=%async_computation.2 | async-start | bytes 2097152 | tf_op jit(solution)/shard_map/all_to_all | solution.py:523
  103.3 0.1 collective-permute-start
  103.4 1.2 collective-permute-done
  104.6 0.6 collective-permute-start.3
  105.3 2.1 %collective-permute-start.2 = (bf16[2,128,256]{2,1,0:T(8,128)(2,1)S(1)}, bf16[2,128,256]{2,1,0:T(8,128)(2,1)S(1)}, u32[]{:S(2)}, u32[]{:S(2)}) collective-permute-start(bf16[2,128,256]{2,1,0:T(8,128)(2,1)S(1)} %pad_maximum_fusion.pair), channel_id=1, source_target_pairs={{0,4},{1,5},{2,6},{3,7},{4,0},{5,1},{6,2},{7,3},{8,12},{9,13},{10,... | collective-permute-start | bytes 393224 | tf_op jit(solution)/shard_map/ppermute | solution.py:529
  107.4 1.4 %collective-permute-start.1 = (bf16[2,128,256]{2,1,0:T(8,128)(2,1)S(1)}, bf16[2,128,256]{2,1,0:T(8,128)(2,1)S(1)}, u32[]{:S(2)}, u32[]{:S(2)}) collective-permute-start(bf16[2,128,256]{2,1,0:T(8,128)(2,1)S(1)} %pad_maximum_fusion.pair), channel_id=1, source_target_pairs={{0,2},{1,3},{2,0},{3,1},{4,6},{5,7},{6,4},{7,5},{8,10},{9,11},{10,... | collective-permute-start | bytes 393224 | tf_op jit(solution)/shard_map/ppermute | solution.py:529
  108.8 5.5 %collective-permute-done.3.refs_2_ = bf16[2,128,256]{2,1,0:T(8,128)(2,1)S(1)} collective-permute-done((bf16[2,128,256]{2,1,0:T(8,128)(2,1)S(1)}, bf16[2,128,256]{2,1,0:T(8,128)(2,1)S(1)}, u32[]{:S(2)}, u32[]{:S(2)}) %collective-permute-start.3) | collective-permute-done | bytes 131104 | tf_op jit(solution)/shard_map/ppermute | solution.py:529
  114.3 0.0 collective-permute-done.2.refs_1_
  114.3 0.6 collective-permute-done.1.refs_0_
  114.9 6.0 %all-to-all-done.2 = bf16[16,128,256]{2,1,0:T(8,128)(2,1)S(1)} async-done(((bf16[16,128,256]{2,1,0:T(8,128)(2,1)}), bf16[16,128,256]{2,1,0:T(8,128)(2,1)S(1)}, u32[]{:S(2)}, u32[]{:S(2)}) %all-to-all-start.2) | async-done | bytes 1048608 | tf_op jit(solution)/shard_map/all_to_all | solution.py:523
  120.9 3.8 %shard_map.118 = f32[1024,2048]{1,0:T(8,128)} custom-call(s32[1]{0:T(128)} %bitcast.me_ref, bf16[2,128,256]{2,1,0:T(8,128)(2,1)S(1)} %pad_maximum_fusion.pair, bf16[2,128,256]{2,1,0:T(8,128)(2,1)S(1)} %collective-permute-done.1.refs_0_, bf16[2,128,256]{2,1,0:T(8,128)(2,1)S(1)} %collective-permute-done.2.refs_1_, ...), custom_call_target="tpu_custom_call" | custom-call | flops 1000000000 | bytes 10000000 | tf_op jit(solution)/shard_map/pallas_call | solution.py:390
  (12 shorter events, 0.0 us)
Async XLA Ops:
  13.2 11.9 %copy-start.9 = (f32[128,8]{0,1:T(8,128)S(1)}, f32[128,8]{0,1:T(8,128)}, u32[]{:S(2)}) copy-start(f32[128,8]{0,1:T(8,128)} %param.18) | copy-start | bytes 12292
  13.2 12.0 %copy-start.10 = (s32[128,8]{0,1:T(8,128)S(1)}, s32[128,8]{0,1:T(8,128)}, u32[]{:S(2)}) copy-start(s32[128,8]{0,1:T(8,128)} %param.19) | copy-start | bytes 12292
  13.2 12.1 %copy-start.2 = (f32[512,512]{1,0:T(8,128)S(1)}, f32[512,512]{1,0:T(8,128)}, u32[]{:S(2)}) copy-start(f32[512,512]{1,0:T(8,128)} %sep_hbm.1) | copy-start | bytes 3145732
  13.2 12.1 %copy-start.4 = (f32[512,256]{1,0:T(8,128)S(1)}, f32[512,256]{1,0:T(8,128)}, u32[]{:S(2)}) copy-start(f32[512,256]{1,0:T(8,128)} %rhs_hbm.1) | copy-start | bytes 1572868
  13.2 41.6 %all-to-all-start = ((bf16[128,32,256]{2,1,0:T(8,128)(2,1)}), bf16[128,32,256]{2,1,0:T(8,128)(2,1)}, u32[]{:S(2)}, u32[]{:S(2)}) async-start(bf16[128,32,256]{2,1,0:T(8,128)(2,1)} %get-tuple-element.13), calls=%async_computation | async-start | bytes 4194304 | tf_op jit(solution)/shard_map/all_to_all | solution.py:451
  25.3 5.6 %copy-start = (f32[1024,1024]{1,0:T(8,128)S(1)}, f32[1024,1024]{1,0:T(8,128)}, u32[]{:S(2)}) copy-start(f32[1024,1024]{1,0:T(8,128)} %factor.3) | copy-start | bytes 12582916
  25.3 5.6 %copy-start.3 = (f32[1024,256]{1,0:T(8,128)S(1)}, f32[1024,256]{1,0:T(8,128)}, u32[]{:S(2)}) copy-start(f32[1024,256]{1,0:T(8,128)} %rhs.3) | copy-start | bytes 3145732
  25.3 5.6 %copy-start.5 = (s32[1,64]{1,0:T(1,128)S(1)}, s32[1,64]{1,0:T(1,128)}, u32[]{:S(2)}) copy-start(s32[1,64]{1,0:T(1,128)} %owner_ref.3) | copy-start | bytes 772
  25.3 5.6 %copy-start.7 = (bf16[2,512,512]{2,1,0:T(8,128)(2,1)S(1)}, bf16[2,512,512]{2,1,0:T(8,128)(2,1)}, u32[]{:S(2)}) copy-start(bf16[2,512,512]{2,1,0:T(8,128)(2,1)} %get-tuple-element.14.high_hbm) | copy-start | bytes 3145732
  25.4 5.6 %copy-start.8 = (bf16[2,512,512]{2,1,0:T(8,128)(2,1)S(1)}, bf16[2,512,512]{2,1,0:T(8,128)(2,1)}, u32[]{:S(2)}) copy-start(bf16[2,512,512]{2,1,0:T(8,128)(2,1)} %get-tuple-element.15.low_hbm) | copy-start | bytes 3145732
  29.7 1.1 copy-start.6
  30.9 2.0 %copy-start.1 = (bf16[1792,1024]{1,0:T(8,128)(2,1)S(1)}, bf16[1792,1024]{1,0:T(8,128)(2,1)}, u32[]{:S(2)}) copy-start(bf16[1792,1024]{1,0:T(8,128)(2,1)} %coupling.3) | copy-start | bytes 11010052
  99.6 21.3 %all-to-all-start.2 = ((bf16[16,128,256]{2,1,0:T(8,128)(2,1)}), bf16[16,128,256]{2,1,0:T(8,128)(2,1)S(1)}, u32[]{:S(2)}, u32[]{:S(2)}) async-start(bf16[16,128,256]{2,1,0:T(8,128)(2,1)} %get-tuple-element.23), calls=%async_computation.2 | async-start | bytes 2097152 | tf_op jit(solution)/shard_map/all_to_all | solution.py:523
  103.3 1.3 %collective-permute-start = (bf16[128,256]{1,0:T(8,128)(2,1)S(1)}, bf16[128,256]{1,0:T(8,128)(2,1)S(1)}, u32[]{:S(2)}, u32[]{:S(2)}) collective-permute-start(bf16[128,256]{1,0:T(8,128)(2,1)S(1)} %get-tuple-element.22), channel_id=1, source_target_pairs={{0,1},{1,0},{2,3},{3,2},{4,5},{5,4},{6,7},{7,6},{8,9},{9,8},{10,11... | collective-permute-start | bytes 196616 | tf_op jit(solution)/shard_map/ppermute | solution.py:526
  104.6 9.7 %collective-permute-start.3 = (bf16[2,128,256]{2,1,0:T(8,128)(2,1)S(1)}, bf16[2,128,256]{2,1,0:T(8,128)(2,1)S(1)}, u32[]{:S(2)}, u32[]{:S(2)}) collective-permute-start(bf16[2,128,256]{2,1,0:T(8,128)(2,1)S(1)} %pad_maximum_fusion.pair), channel_id=1, source_target_pairs={{0,6},{1,7},{2,4},{3,5},{4,2},{5,3},{6,0},{7,1},{8,14},{9,15},{10,... | collective-permute-start | bytes 393224 | tf_op jit(solution)/shard_map/ppermute | solution.py:529
  105.3 9.0 %collective-permute-start.2 = (bf16[2,128,256]{2,1,0:T(8,128)(2,1)S(1)}, bf16[2,128,256]{2,1,0:T(8,128)(2,1)S(1)}, u32[]{:S(2)}, u32[]{:S(2)}) collective-permute-start(bf16[2,128,256]{2,1,0:T(8,128)(2,1)S(1)} %pad_maximum_fusion.pair), channel_id=1, source_target_pairs={{0,4},{1,5},{2,6},{3,7},{4,0},{5,1},{6,2},{7,3},{8,12},{9,13},{10,... | collective-permute-start | bytes 393224 | tf_op jit(solution)/shard_map/ppermute | solution.py:529
  107.4 7.6 %collective-permute-start.1 = (bf16[2,128,256]{2,1,0:T(8,128)(2,1)S(1)}, bf16[2,128,256]{2,1,0:T(8,128)(2,1)S(1)}, u32[]{:S(2)}, u32[]{:S(2)}) collective-permute-start(bf16[2,128,256]{2,1,0:T(8,128)(2,1)S(1)} %pad_maximum_fusion.pair), channel_id=1, source_target_pairs={{0,2},{1,3},{2,0},{3,1},{4,6},{5,7},{6,4},{7,5},{8,10},{9,11},{10,... | collective-permute-start | bytes 393224 | tf_op jit(solution)/shard_map/ppermute | solution.py:529

commit v4 on v3

--- a/solution.py
+++ b/solution.py
@@ -12,7 +12,6 @@
 UNIT = 128
 BASE = 256
 WIDE = 512
-FULL = 60.5
 PAD = 32
 LANES = 128
 VMEM = pltpu.VMEM
@@ -125,13 +124,19 @@
         copy.wait()
 
 
-def place_rows(source, target, owner_ref, count, slots, halves, extra=None):
+def place_rows(source, target, owner_ref, count, slots, halves, extra=None, again=0):
     width = target.shape[2]
+    spare = PAD - slots
     row = lax.broadcasted_iota(jnp.int32, (PAD, width), 0)
     for j in range(halves):
         live = jnp.minimum(count - slots * j, slots)
-        rows = source[slots * j : slots * j + PAD, :]
-        rows = jnp.where(row < live, rows, 0.0)
+        first = slots * j + again
+        rows = source[first : first + PAD, :]
+        keep = row < live
+        if again:
+            rows = jnp.where(row < slots, rows, source[first - spare : first - spare + PAD, :])
+            keep = jnp.where(row < slots, row, row - spare) < live
+        rows = jnp.where(keep, rows, 0.0)
         if extra is not None:
             rows = jnp.where(row == slots, extra[j : j + 1, :], rows)
         target[owner_ref[0, j]] = rows.astype(target.dtype)
@@ -283,9 +288,10 @@
     both = mm(block[:, :half], jnp.concatenate(y0, axis=0), NT) + mm(
         block[:, half:], jnp.concatenate(y1, axis=0), NT
     )
-    rows[:bound, :] = both[:, :cells] + both[:, cells:]
-    rows[bound:, :] = jnp.zeros((rows.shape[0] - bound, cells), F32)
-    place_rows(rows, placed, owner_ref, count_ref[0], bound // halves, halves)
+    rows[:8, :] = jnp.zeros((8, cells), F32)
+    rows[8 : 8 + bound, :] = both[:, :cells] + both[:, cells:]
+    rows[8 + bound :, :] = jnp.zeros((rows.shape[0] - bound - 8, cells), F32)
+    place_rows(rows, placed, owner_ref, count_ref[0], bound // halves, halves, again=8)
     group = LANES // PAD
     for t in range(placed.shape[0] // group):
         tile = placed[t * group : (t + 1) * group].reshape(LANES, cells).T
@@ -296,8 +302,32 @@
     return jnp.where(cond, jnp.ones((), BF16), jnp.zeros((), BF16))
 
 
+def fold_halves(blocks, slots):
+    left, right = blocks[:, :, :LANES], blocks[:, :, LANES:]
+    whole = slots // 8 * 8
+    pieces = []
+    for top in range(0, whole, 8):
+        pieces += [left[:, top : top + 8], right[:, top : top + 8]]
+    row = lax.broadcasted_iota(jnp.int32, (blocks.shape[0], 8, LANES), 1)
+    pieces.append(jnp.where(row < slots - whole, left[:, whole:], right[:, whole:]))
+    return jnp.concatenate(pieces, axis=1)
+
+
+def unfold_halves(folded, slots):
+    whole = slots // 8 * 8
+    shared = folded[:, 2 * whole :]
+    row = lax.broadcasted_iota(jnp.int32, shared.shape, 1)
+    left = [folded[:, 2 * top : 2 * top + 8] for top in range(0, whole, 8)]
+    right = [folded[:, 2 * top + 8 : 2 * top + 16] for top in range(0, whole, 8)]
+    left.append(jnp.where(row < slots - whole, shared, 0.0))
+    right.append(jnp.where(row < slots - whole, 0.0, shared))
+    return jnp.concatenate(
+        [jnp.concatenate(left, axis=1), jnp.concatenate(right, axis=1)], axis=2
+    )
+
+
 def separator_kernel(
-    incoming, schur_hbm, potential_hbm, replies_hbm, schur, potential, replies, sems, *, slots
+    incoming, schur_hbm, potential, replies, schur, sems, *, slots
 ):
     fronts = incoming.shape[0]
     chunks = fronts * PAD // WIDE
@@ -312,7 +342,10 @@
     low_bits, high_bits = tail[:, :LANES], tail[:, LANES:]
     rows = [jnp.where(high_bits == 1.0 + p, low_bits, -1.0) for p in range(2)]
     empty = jnp.full((LANES - rows[0].shape[0], LANES), -1.0, F32)
-    cols = [jnp.concatenate([one, empty], axis=0).T for one in rows]
+    spare = PAD - slots
+    last = (lax.broadcasted_iota(jnp.int32, rows[0].shape, 1) & (PAD - 1)) >= slots
+    twice = [jnp.where(last, pltpu.roll(one, spare, 1), one) for one in rows]
+    cols = [jnp.concatenate([one, empty], axis=0).T for one in twice]
     order = schur.shape[0]
     part = order // 2
     down = lax.broadcasted_iota(jnp.int32, (part, LANES), 0).astype(F32).astype(BF16)
@@ -332,8 +365,6 @@
     wait(rest)
     found = mm3(split(schur[:, :order]), split(schur[:, order:] - total))
     potential[...] = found
-    stores = copy_all([(potential, potential_hbm)], sems)
-    start(stores)
     rounded = found.astype(BF16)
     for c in range(chunks):
         tiles = [
@@ -343,19 +374,13 @@
             for g in range(c * each, (c + 1) * each)
         ]
         chosen = jnp.concatenate(tiles, axis=0)
-        replies[c * per : (c + 1) * per] = (
-            mm(chosen, rounded).astype(BF16).reshape(per, PAD, rounded.shape[1])
-        )
-        if (c + 1) % (chunks // 2) == 0:
-            first = (c + 1 - chunks // 2) * per
-            last = (c + 1) * per
-            stores += copy_all([(replies.at[first:last], replies_hbm.at[first:last])], sems, 1 + c)
-            stores[-1].start()
-    wait(stores)
-
-
-def field_kernel(field0, g_high, g_low, returned, field, spread):
-    values = returned[...]
+        blocks = mm(chosen, rounded).reshape(per, PAD, rounded.shape[1])
+        replies[c * per : (c + 1) * per] = fold_halves(blocks, slots).astype(BF16)
+
+
+def field_kernel(field0, g_high, g_low, returned, field, spread, *, slots):
+    values = unfold_halves(returned[...].astype(F32), slots).astype(BF16)
+    values = values.reshape(g_high.shape[1], -1)
     found = (field0[...] - (mm(g_high[...], values) + mm(g_low[...], values))).astype(BF16)
     field[...] = found
     for r in range(spread.shape[0]):
@@ -411,6 +436,7 @@
     halves = sep_owner.shape[1]
     cells = cell_weight.shape[0]
     half = order // 2
+    slots = bound // halves
     flat = fronts * PAD
     vm = pl.BlockSpec(memory_space=VMEM)
     sm = pl.BlockSpec(memory_space=SMEM)
@@ -481,7 +507,7 @@
             VMEM((bound, order), BF16),
             VMEM((2, half, half), BF16),
             VMEM((2, half, half), BF16),
-            VMEM((bound + 8, cells), F32),
+            VMEM((bound + 16, cells), F32),
             VMEM((fronts, PAD, cells), F32),
             dma((5,)),
         ],
@@ -493,24 +519,22 @@
     )
     schur, _ = lax.optimization_barrier((schur, g_high))
     sep_potential, replies = call(
-        lambda *refs: separator_kernel(*refs, slots=bound // halves),
-        (shape((sep_size, sources), F32), shape((fronts, PAD, sources), BF16)),
+        lambda *refs: separator_kernel(*refs, slots=slots),
+        (shape((sep_size, sources), F32), shape((fronts, 2 * slots, LANES), BF16)),
         (incoming, schur),
         [
             VMEM((sep_size, sep_size + sources), F32),
-            VMEM((sep_size, sources), F32),
-            VMEM((fronts, PAD, sources), BF16),
-            dma((flat // WIDE + 1,)),
+            dma((1,)),
         ],
         [vm, hbm],
-        (hbm, hbm),
+        (vm, vm),
         3_000_000_000,
         5_000_000,
-        FULL,
-    )
-    returned = exchange(replies).reshape(flat, sources)
+        28,
+    )
+    returned = exchange(replies)
     field, spread = call(
-        field_kernel,
+        lambda *refs: field_kernel(*refs, slots=slots),
         (shape((cells, sources), BF16), shape((row_count, cells, sources), BF16)),
         (field0, g_high, g_low, returned),
         [],

time: 125 us -> 121 us (0.968)
  blocking collectives: 35.5 us -> 31.9 us
  local copies, waits for them, and re-layouts: 3.43 us -> 6.86 us
  Pallas kernels: 36.9 us -> 34.4 us
  waiting for transfers between devices: 27.7 us -> 26.1 us
    all_to_all x1, blocking collectives: 35.5 us -> 31.9 us  [exchange(): return lax.all_to_all(blocks, both, split_axis=0, concat_axis=0, tiled=True)]
    unnamed x24 -> x30, local copies, waits for them, and re-layouts: 3.43 us -> 6.86 us
    pallas_call x6, Pallas kernels: 36.9 us -> 34.4 us  [call(): pl.pallas_call(kernel, out_shape=outs, in_specs=specs, out_specs=out_spec...]
    all_to_all x1, waiting for transfers between devices: 14.3 us -> 12.7 us  [exchange(): return lax.all_to_all(blocks, both, split_axis=0, concat_axis=0, tiled=True)]
where the time goes in v4:
time: 121 us; the launch traced here: 120 us
  Pallas kernels  34.4 us (28%)
  blocking collectives  31.9 us (26%)
  waiting for transfers between devices  26.1 us (22%)
  starting transfers between devices  19.2 us (16%)
  local copies, waits for them, and re-layouts  6.86 us (6%)
  between operations  1.63 us (1%)
    pallas_call x6, Pallas kernels, call(): pl.pallas_call(kernel, out_shape=outs, in_specs=specs, out_specs=out_spec...  34.4 us
    all_to_all x1, blocking collectives, exchange(): return lax.all_to_all(blocks, both, split_axis=0, concat_axis=0, tiled=True)  31.9 us
    all_to_all x1, waiting for transfers between devices, exchange(): return lax.all_to_all(blocks, both, split_axis=0, concat_axis=0, tiled=True)  12.7 us
    all_to_all x1, starting transfers between devices, exchange(): return lax.all_to_all(blocks, both, split_axis=0, concat_axis=0, tiled=True)  11.3 us
    unnamed x30, local copies, waits for them, and re-layouts  6.86 us
    all_to_all x1, waiting for transfers between devices, local(): lax.all_to_all(spread, 'row', split_axis=0, concat_axis=0, tiled=True)  6.1 us
    ppermute x3, waiting for transfers between devices, local(): lax.ppermute(pair, 'col', [(i, i ^ 2 * d) for i in range(col_count)])  6.07 us
    ppermute x3, starting transfers between devices, local(): lax.ppermute(pair, 'col', [(i, i ^ 2 * d) for i in range(col_count)])  4.17 us
  transfers between devices with their start and end apart: 6, of which 5 were waited for; matrix products, arithmetic and copies ran while one was open for 0% of the time, Pallas kernels for 10%

profile of v4, /device:TPU:0, one launch (start us, length us, event | category | flops | bytes accessed | tf_op | source)
XLA Modules:
  0.0 120.2 jit_solution(9601764242590045169)
XLA Ops:
  1.3 11.9 %shard_map.113 = (bf16[128,32,256]{2,1,0:T(8,128)(2,1)}, bf16[2,512,512]{2,1,0:T(8,128)(2,1)}, bf16[2,512,512]{2,1,0:T(8,128)(2,1)}) custom-call(s32[1,64]{1,0:T(1,128)} %owner_ref.3, s32[1]{0:T(128)S(6)} %copy.14.count_ref, s32[1]{0:T(128)} %bitcast.me_ref, s32[1,1792]{1,0:T(1,128)} %index.1, f32[1024,1024]{1,0:T(8,128)} %factor.3, f32[1024,256]{1,0:T(8,128)} %rhs.3, ...), custom_call_target="tpu_custom_call" | custom-call | flops 8000000000 | bytes 14000000 | tf_op jit(solution)/shard_map/pallas_call | solution.py:415
  13.2 0.0 copy-start.12
  13.2 0.0 copy-start.13
  13.2 0.0 copy-start.4
  13.2 11.3 %all-to-all-start = ((bf16[128,32,256]{2,1,0:T(8,128)(2,1)}), bf16[128,32,256]{2,1,0:T(8,128)(2,1)S(1)}, u32[]{:S(2)}, u32[]{:S(2)}) async-start(bf16[128,32,256]{2,1,0:T(8,128)(2,1)} %get-tuple-element.13), calls=%async_computation | async-start | bytes 4194304 | tf_op jit(solution)/shard_map/all_to_all | solution.py:477
  24.5 0.1 copy.12.weight
  24.6 0.0 copy-done.13
  24.6 0.1 copy.13.pivot
  24.8 0.0 copy-start.6
  24.8 1.0 copy-done.6
  25.8 4.4 %shard_map.114.refs_1_ = f32[512,768]{1,0:T(8,128)S(1)} custom-call(f32[512,512]{1,0:T(8,128)S(1)} %copy-done.4, f32[512,256]{1,0:T(8,128)S(1)} %copy-done.6), custom_call_target="tpu_custom_call" | custom-call | flops 2000000000 | bytes 3000000 | tf_op jit(solution)/shard_map/pallas_call | solution.py:415
  30.2 1.2 copy-done.8
  31.4 0.0 copy-start.3
  31.4 2.0 %copy-done.3 = bf16[1792,1024]{1,0:T(8,128)(2,1)S(1)} copy-done((bf16[1792,1024]{1,0:T(8,128)(2,1)S(1)}, bf16[1792,1024]{1,0:T(8,128)(2,1)}, u32[]{:S(2)}) %copy-start.3) | copy-done | bytes 3670040
  33.4 7.6 %shard_map.115 = (f32[128,256]{1,0:T(8,128)S(1)}, bf16[128,4096]{1,0:T(8,128)(2,1)S(1)}, bf16[128,4096]{1,0:T(8,128)(2,1)S(1)}) custom-call(s32[1,64]{1,0:T(1,128)S(1)} %copy-done.7, s32[1]{0:T(128)S(6)} %copy.14.count_ref, f32[1024,1024]{1,0:T(8,128)S(1)} %copy-done.2, f32[1024,256]{1,0:T(8,128)S(1)} %copy-done.5, bf16[1792,1024]{1,0:T(8,128)(2,1)S(1)} %copy-done.3, ...), custom_call_target="tpu_custom_call" | custom-call | flops 4000000000 | bytes 11000000 | tf_op jit(solution)/shard_map/pallas_call | solution.py:415
  41.1 1.0 copy-done
  42.0 12.7 %all-to-all-done.refs_0_ = bf16[128,32,256]{2,1,0:T(8,128)(2,1)S(1)} async-done(((bf16[128,32,256]{2,1,0:T(8,128)(2,1)}), bf16[128,32,256]{2,1,0:T(8,128)(2,1)S(1)}, u32[]{:S(2)}, u32[]{:S(2)}) %all-to-all-start) | async-done | bytes 2097184 | tf_op jit(solution)/shard_map/all_to_all | solution.py:477
  54.7 1.4 %copy-done.9 = f32[512,768]{1,0:T(8,128)S(1)} copy-done((f32[512,768]{1,0:T(8,128)S(1)}, f32[512,768]{1,0:T(8,128)}, u32[]{:S(2)}) %copy-start.9) | copy-done | bytes 1572888
  56.1 5.0 %shard_map.116 = (f32[512,256]{1,0:T(8,128)}, bf16[128,56,128]{2,1,0:T(8,128)(2,1)S(1)}) custom-call(bf16[128,32,256]{2,1,0:T(8,128)(2,1)S(1)} %all-to-all-done.refs_0_, f32[512,768]{1,0:T(8,128)S(1)} %copy-done.9), custom_call_target="tpu_custom_call" | custom-call | flops 3000000000 | bytes 5000000 | tf_op jit(solution)/shard_map/pallas_call | solution.py:415
  61.1 31.9 %all_to_all.15.refs_3_ = bf16[128,56,128]{2,1,0:T(8,128)(2,1)S(1)} all-to-all(bf16[128,56,128]{2,1,0:T(8,128)(2,1)S(1)} %get-tuple-element.21), channel_id=1, replica_groups=mesh['row'=16,'col'=8] {'row','col'}, dimensions={0} | all-to-all | bytes 3670016 | tf_op jit(solution)/shard_map/all_to_all | solution.py:477
  93.1 1.8 %shard_map.117 = (bf16[128,256]{1,0:T(8,128)(2,1)S(1)}, bf16[16,128,256]{2,1,0:T(8,128)(2,1)}) custom-call(f32[128,256]{1,0:T(8,128)S(1)} %get-tuple-element.19.refs_0_, bf16[128,4096]{1,0:T(8,128)(2,1)S(1)} %get-tuple-element.16.refs_1_, bf16[128,4096]{1,0:T(8,128)(2,1)S(1)} %copy-done.1, bf16[128,56,128]{2,1,0:T(8,128)(2,1)S(1)} %all_to_all.15.refs_3_), custom_call_target="tpu_custom_call" | custom-call | flops 600000000 | bytes 5000000 | tf_op jit(solution)/shard_map/pallas_call | solution.py:415
  94.8 3.7 %all-to-all-start.2 = ((bf16[16,128,256]{2,1,0:T(8,128)(2,1)}), bf16[16,128,256]{2,1,0:T(8,128)(2,1)S(1)}, u32[]{:S(2)}, u32[]{:S(2)}) async-start(bf16[16,128,256]{2,1,0:T(8,128)(2,1)} %get-tuple-element.23), calls=%async_computation.2 | async-start | bytes 2097152 | tf_op jit(solution)/shard_map/all_to_all | solution.py:547
  98.5 0.1 collective-permute-start
  98.6 1.2 %collective-permute-done = bf16[128,256]{1,0:T(8,128)(2,1)S(1)} collective-permute-done((bf16[128,256]{1,0:T(8,128)(2,1)S(1)}, bf16[128,256]{1,0:T(8,128)(2,1)S(1)}, u32[]{:S(2)}, u32[]{:S(2)}) %collective-permute-start) | collective-permute-done | bytes 65568 | tf_op jit(solution)/shard_map/ppermute | solution.py:550
  99.8 0.6 collective-permute-start.3
  100.4 2.1 %collective-permute-start.2 = (bf16[2,128,256]{2,1,0:T(8,128)(2,1)S(1)}, bf16[2,128,256]{2,1,0:T(8,128)(2,1)S(1)}, u32[]{:S(2)}, u32[]{:S(2)}) collective-permute-start(bf16[2,128,256]{2,1,0:T(8,128)(2,1)S(1)} %pad_maximum_fusion.pair), channel_id=1, source_target_pairs={{0,4},{1,5},{2,6},{3,7},{4,0},{5,1},{6,2},{7,3},{8,12},{9,13},{10,... | collective-permute-start | bytes 393224 | tf_op jit(solution)/shard_map/ppermute | solution.py:553
  102.6 1.4 %collective-permute-start.1 = (bf16[2,128,256]{2,1,0:T(8,128)(2,1)S(1)}, bf16[2,128,256]{2,1,0:T(8,128)(2,1)S(1)}, u32[]{:S(2)}, u32[]{:S(2)}) collective-permute-start(bf16[2,128,256]{2,1,0:T(8,128)(2,1)S(1)} %pad_maximum_fusion.pair), channel_id=1, source_target_pairs={{0,2},{1,3},{2,0},{3,1},{4,6},{5,7},{6,4},{7,5},{8,10},{9,11},{10,... | collective-permute-start | bytes 393224 | tf_op jit(solution)/shard_map/ppermute | solution.py:553
  104.0 5.5 %collective-permute-done.3.refs_2_ = bf16[2,128,256]{2,1,0:T(8,128)(2,1)S(1)} collective-permute-done((bf16[2,128,256]{2,1,0:T(8,128)(2,1)S(1)}, bf16[2,128,256]{2,1,0:T(8,128)(2,1)S(1)}, u32[]{:S(2)}, u32[]{:S(2)}) %collective-permute-start.3) | collective-permute-done | bytes 131104 | tf_op jit(solution)/shard_map/ppermute | solution.py:553
  109.5 0.0 collective-permute-done.2.refs_1_
  109.5 0.6 collective-permute-done.1.refs_0_
  110.1 6.1 %all-to-all-done.2 = bf16[16,128,256]{2,1,0:T(8,128)(2,1)S(1)} async-done(((bf16[16,128,256]{2,1,0:T(8,128)(2,1)}), bf16[16,128,256]{2,1,0:T(8,128)(2,1)S(1)}, u32[]{:S(2)}, u32[]{:S(2)}) %all-to-all-start.2) | async-done | bytes 1048608 | tf_op jit(solution)/shard_map/all_to_all | solution.py:547
  116.2 3.8 %shard_map.118 = f32[1024,2048]{1,0:T(8,128)} custom-call(s32[1]{0:T(128)} %bitcast.me_ref, bf16[2,128,256]{2,1,0:T(8,128)(2,1)S(1)} %pad_maximum_fusion.pair, bf16[2,128,256]{2,1,0:T(8,128)(2,1)S(1)} %collective-permute-done.1.refs_0_, bf16[2,128,256]{2,1,0:T(8,128)(2,1)S(1)} %collective-permute-done.2.refs_1_, ...), custom_call_target="tpu_custom_call" | custom-call | flops 1000000000 | bytes 10000000 | tf_op jit(solution)/shard_map/pallas_call | solution.py:415
  (18 shorter events, 0.0 us)
Async XLA Ops:
  13.2 11.4 %copy-start.12 = (f32[128,8]{0,1:T(8,128)S(1)}, f32[128,8]{0,1:T(8,128)}, u32[]{:S(2)}) copy-start(f32[128,8]{0,1:T(8,128)} %param.18) | copy-start | bytes 12292
  13.2 11.5 %copy-start.13 = (s32[128,8]{0,1:T(8,128)S(1)}, s32[128,8]{0,1:T(8,128)}, u32[]{:S(2)}) copy-start(s32[128,8]{0,1:T(8,128)} %param.19) | copy-start | bytes 12292
  13.2 11.6 %copy-start.4 = (f32[512,512]{1,0:T(8,128)S(1)}, f32[512,512]{1,0:T(8,128)}, u32[]{:S(2)}) copy-start(f32[512,512]{1,0:T(8,128)} %sep_hbm.1) | copy-start | bytes 3145732
  13.2 41.5 %all-to-all-start = ((bf16[128,32,256]{2,1,0:T(8,128)(2,1)}), bf16[128,32,256]{2,1,0:T(8,128)(2,1)S(1)}, u32[]{:S(2)}, u32[]{:S(2)}) async-start(bf16[128,32,256]{2,1,0:T(8,128)(2,1)} %get-tuple-element.13), calls=%async_computation | async-start | bytes 4194304 | tf_op jit(solution)/shard_map/all_to_all | solution.py:477
  24.8 1.0 copy-start.6
  25.8 5.6 %copy-start.2 = (f32[1024,1024]{1,0:T(8,128)S(1)}, f32[1024,1024]{1,0:T(8,128)}, u32[]{:S(2)}) copy-start(f32[1024,1024]{1,0:T(8,128)} %factor.3) | copy-start | bytes 12582916
  25.8 5.6 %copy-start.5 = (f32[1024,256]{1,0:T(8,128)S(1)}, f32[1024,256]{1,0:T(8,128)}, u32[]{:S(2)}) copy-start(f32[1024,256]{1,0:T(8,128)} %rhs.3) | copy-start | bytes 3145732
  25.8 5.6 %copy-start.7 = (s32[1,64]{1,0:T(1,128)S(1)}, s32[1,64]{1,0:T(1,128)}, u32[]{:S(2)}) copy-start(s32[1,64]{1,0:T(1,128)} %owner_ref.3) | copy-start | bytes 772
  25.8 5.6 %copy-start.10 = (bf16[2,512,512]{2,1,0:T(8,128)(2,1)S(1)}, bf16[2,512,512]{2,1,0:T(8,128)(2,1)}, u32[]{:S(2)}) copy-start(bf16[2,512,512]{2,1,0:T(8,128)(2,1)} %get-tuple-element.14.high_hbm) | copy-start | bytes 3145732
  25.8 5.6 %copy-start.11 = (bf16[2,512,512]{2,1,0:T(8,128)(2,1)S(1)}, bf16[2,512,512]{2,1,0:T(8,128)(2,1)}, u32[]{:S(2)}) copy-start(bf16[2,512,512]{2,1,0:T(8,128)(2,1)} %get-tuple-element.15.low_hbm) | copy-start | bytes 3145732
  30.2 1.2 copy-start.8
  31.4 2.0 %copy-start.3 = (bf16[1792,1024]{1,0:T(8,128)(2,1)S(1)}, bf16[1792,1024]{1,0:T(8,128)(2,1)}, u32[]{:S(2)}) copy-start(bf16[1792,1024]{1,0:T(8,128)(2,1)} %coupling.3) | copy-start | bytes 11010052
  41.0 1.0 copy-start
  54.7 1.4 %copy-start.9 = (f32[512,768]{1,0:T(8,128)S(1)}, f32[512,768]{1,0:T(8,128)}, u32[]{:S(2)}) copy-start(f32[512,768]{1,0:T(8,128)} %copy-done.8) | copy-start | bytes 4718596
  61.1 31.9 %copy-start.1 = (bf16[128,4096]{1,0:T(8,128)(2,1)S(1)}, bf16[128,4096]{1,0:T(8,128)(2,1)}, u32[]{:S(2)}) copy-start(bf16[128,4096]{1,0:T(8,128)(2,1)} %copy-done) | copy-start | bytes 3145732
  94.8 21.4 %all-to-all-start.2 = ((bf16[16,128,256]{2,1,0:T(8,128)(2,1)}), bf16[16,128,256]{2,1,0:T(8,128)(2,1)S(1)}, u32[]{:S(2)}, u32[]{:S(2)}) async-start(bf16[16,128,256]{2,1,0:T(8,128)(2,1)} %get-tuple-element.23), calls=%async_computation.2 | async-start | bytes 2097152 | tf_op jit(solution)/shard_map/all_to_all | solution.py:547
  98.5 1.3 %collective-permute-start = (bf16[128,256]{1,0:T(8,128)(2,1)S(1)}, bf16[128,256]{1,0:T(8,128)(2,1)S(1)}, u32[]{:S(2)}, u32[]{:S(2)}) collective-permute-start(bf16[128,256]{1,0:T(8,128)(2,1)S(1)} %get-tuple-element.22), channel_id=1, source_target_pairs={{0,1},{1,0},{2,3},{3,2},{4,5},{5,4},{6,7},{7,6},{8,9},{9,8},{10,11... | collective-permute-start | bytes 196616 | tf_op jit(solution)/shard_map/ppermute | solution.py:550
  99.8 9.7 %collective-permute-start.3 = (bf16[2,128,256]{2,1,0:T(8,128)(2,1)S(1)}, bf16[2,128,256]{2,1,0:T(8,128)(2,1)S(1)}, u32[]{:S(2)}, u32[]{:S(2)}) collective-permute-start(bf16[2,128,256]{2,1,0:T(8,128)(2,1)S(1)} %pad_maximum_fusion.pair), channel_id=1, source_target_pairs={{0,6},{1,7},{2,4},{3,5},{4,2},{5,3},{6,0},{7,1},{8,14},{9,15},{10,... | collective-permute-start | bytes 393224 | tf_op jit(solution)/shard_map/ppermute | solution.py:553
  100.4 9.1 %collective-permute-start.2 = (bf16[2,128,256]{2,1,0:T(8,128)(2,1)S(1)}, bf16[2,128,256]{2,1,0:T(8,128)(2,1)S(1)}, u32[]{:S(2)}, u32[]{:S(2)}) collective-permute-start(bf16[2,128,256]{2,1,0:T(8,128)(2,1)S(1)} %pad_maximum_fusion.pair), channel_id=1, source_target_pairs={{0,4},{1,5},{2,6},{3,7},{4,0},{5,1},{6,2},{7,3},{8,12},{9,13},{10,... | collective-permute-start | bytes 393224 | tf_op jit(solution)/shard_map/ppermute | solution.py:553
  102.6 7.5 %collective-permute-start.1 = (bf16[2,128,256]{2,1,0:T(8,128)(2,1)S(1)}, bf16[2,128,256]{2,1,0:T(8,128)(2,1)S(1)}, u32[]{:S(2)}, u32[]{:S(2)}) collective-permute-start(bf16[2,128,256]{2,1,0:T(8,128)(2,1)S(1)} %pad_maximum_fusion.pair), channel_id=1, source_target_pairs={{0,2},{1,3},{2,0},{3,1},{4,6},{5,7},{6,4},{7,5},{8,10},{9,11},{10,... | collective-permute-start | bytes 393224 | tf_op jit(solution)/shard_map/ppermute | solution.py:553

commit v5 on v4

--- a/solution.py
+++ b/solution.py
@@ -257,7 +257,7 @@
 
 def project_kernel(
     owner_ref, count_ref, factor, rhs, coupling, high_hbm, low_hbm, weight, pivot,
-    field0, g_high, g_low,
+    field0, weights,
     lower, right, block, high, low, rows, placed, sems,
 ):
     half = lower.shape[0]
@@ -295,7 +295,7 @@
     group = LANES // PAD
     for t in range(placed.shape[0] // group):
         tile = placed[t * group : (t + 1) * group].reshape(LANES, cells).T
-        g_high[:, t * LANES : (t + 1) * LANES], g_low[:, t * LANES : (t + 1) * LANES] = split(tile)
+        weights[:, t * LANES : (t + 1) * LANES] = jnp.concatenate(split(tile), axis=0)
 
 
 def pick(cond):
@@ -378,10 +378,12 @@
         replies[c * per : (c + 1) * per] = fold_halves(blocks, slots).astype(BF16)
 
 
-def field_kernel(field0, g_high, g_low, returned, field, spread, *, slots):
+def field_kernel(field0, weights, returned, field, spread, *, slots):
     values = unfold_halves(returned[...].astype(F32), slots).astype(BF16)
-    values = values.reshape(g_high.shape[1], -1)
-    found = (field0[...] - (mm(g_high[...], values) + mm(g_low[...], values))).astype(BF16)
+    values = values.reshape(weights.shape[1], -1)
+    cells = field0.shape[0]
+    both = mm(weights[...], values)
+    found = (field0[...] - (both[:cells] + both[cells:])).astype(BF16)
     field[...] = found
     for r in range(spread.shape[0]):
         spread[r] = found
@@ -490,12 +492,11 @@
         3_000_000,
         24,
     )
-    field0, g_high, g_low = call(
+    field0, weights = call(
         project_kernel,
         (
             shape((cells, sources), F32),
-            shape((cells, flat), BF16),
-            shape((cells, flat), BF16),
+            shape((2 * cells, flat), BF16),
         ),
         (
             sep_owner, bound_count, front_factor, rhs, coupling, inv_high, inv_low,
@@ -512,12 +513,12 @@
             dma((5,)),
         ],
         [sm, sm, hbm, hbm, hbm, hbm, hbm, vm, vm],
-        (vm,) * 3,
+        (vm,) * 2,
         4_000_000_000,
         11_000_000,
         36,
     )
-    schur, _ = lax.optimization_barrier((schur, g_high))
+    schur, _ = lax.optimization_barrier((schur, weights))
     sep_potential, replies = call(
         lambda *refs: separator_kernel(*refs, slots=slots),
         (shape((sep_size, sources), F32), shape((fronts, 2 * slots, LANES), BF16)),
@@ -536,9 +537,9 @@
     field, spread = call(
         lambda *refs: field_kernel(*refs, slots=slots),
         (shape((cells, sources), BF16), shape((row_count, cells, sources), BF16)),
-        (field0, g_high, g_low, returned),
+        (field0, weights, returned),
         [],
-        [vm] * 4,
+        [vm] * 3,
         (vm, vm),
         600_000_000,
         5_000_000,

time: 121 us -> 121 us (level)
  no operation moved by 1% of the time
where the time goes in v5:
time: 121 us; the launch traced here: 120 us
  Pallas kernels  34.4 us (28%)
  blocking collectives  31.9 us (26%)
  waiting for transfers between devices  25.8 us (21%)
  starting transfers between devices  19.2 us (16%)
  local copies, waits for them, and re-layouts  7.18 us (6%)
  between operations  1.63 us (1%)
    pallas_call x6, Pallas kernels, call(): pl.pallas_call(kernel, out_shape=outs, in_specs=specs, out_specs=out_spec...  34.4 us
    all_to_all x1, blocking collectives, exchange(): return lax.all_to_all(blocks, both, split_axis=0, concat_axis=0, tiled=True)  31.9 us
    all_to_all x1, waiting for transfers between devices, exchange(): return lax.all_to_all(blocks, both, split_axis=0, concat_axis=0, tiled=True)  12.4 us
    all_to_all x1, starting transfers between devices, exchange(): return lax.all_to_all(blocks, both, split_axis=0, concat_axis=0, tiled=True)  11.3 us
    unnamed x30, local copies, waits for them, and re-layouts  7.18 us
    all_to_all x1, waiting for transfers between devices, local(): lax.all_to_all(spread, 'row', split_axis=0, concat_axis=0, tiled=True)  6.1 us
    ppermute x3, waiting for transfers between devices, local(): lax.ppermute(pair, 'col', [(i, i ^ 2 * d) for i in range(col_count)])  6.07 us
    ppermute x3, starting transfers between devices, local(): lax.ppermute(pair, 'col', [(i, i ^ 2 * d) for i in range(col_count)])  4.17 us
  transfers between devices with their start and end apart: 6, of which 5 were waited for; matrix products, arithmetic and copies ran while one was open for 0% of the time, Pallas kernels for 10%

profile of v5, /device:TPU:0, one launch (start us, length us, event | category | flops | bytes accessed | tf_op | source)
XLA Modules:
  0.0 120.2 jit_solution(17011792101550611413)
XLA Ops:
  1.3 11.9 %shard_map.113 = (bf16[128,32,256]{2,1,0:T(8,128)(2,1)}, bf16[2,512,512]{2,1,0:T(8,128)(2,1)}, bf16[2,512,512]{2,1,0:T(8,128)(2,1)}) custom-call(s32[1,64]{1,0:T(1,128)} %owner_ref.3, s32[1]{0:T(128)S(6)} %copy.14.count_ref, s32[1]{0:T(128)} %bitcast.me_ref, s32[1,1792]{1,0:T(1,128)} %index.1, f32[1024,1024]{1,0:T(8,128)} %factor.3, f32[1024,256]{1,0:T(8,128)} %rhs.3, ...), custom_call_target="tpu_custom_call" | custom-call | flops 8000000000 | bytes 14000000 | tf_op jit(solution)/shard_map/pallas_call | solution.py:417
  13.2 0.0 copy-start.12
  13.2 0.0 copy-start.13
  13.2 0.0 copy-start.4
  13.2 11.3 %all-to-all-start = ((bf16[128,32,256]{2,1,0:T(8,128)(2,1)}), bf16[128,32,256]{2,1,0:T(8,128)(2,1)S(1)}, u32[]{:S(2)}, u32[]{:S(2)}) async-start(bf16[128,32,256]{2,1,0:T(8,128)(2,1)} %get-tuple-element.12), calls=%async_computation | async-start | bytes 4194304 | tf_op jit(solution)/shard_map/all_to_all | solution.py:479
  24.5 0.1 copy.12.weight
  24.6 0.0 copy-done.13
  24.6 0.1 copy.13.pivot
  24.8 0.0 copy-start.6
  24.8 1.0 copy-done.6
  25.8 4.4 %shard_map.114.refs_1_ = f32[512,768]{1,0:T(8,128)S(1)} custom-call(f32[512,512]{1,0:T(8,128)S(1)} %copy-done.4, f32[512,256]{1,0:T(8,128)S(1)} %copy-done.6), custom_call_target="tpu_custom_call" | custom-call | flops 2000000000 | bytes 3000000 | tf_op jit(solution)/shard_map/pallas_call | solution.py:417
  30.2 1.1 copy-done.8
  31.4 0.0 copy-start.3
  31.4 2.0 %copy-done.3 = bf16[1792,1024]{1,0:T(8,128)(2,1)S(1)} copy-done((bf16[1792,1024]{1,0:T(8,128)(2,1)S(1)}, bf16[1792,1024]{1,0:T(8,128)(2,1)}, u32[]{:S(2)}) %copy-start.3) | copy-done | bytes 3670040
  33.4 7.6 %shard_map.115 = (f32[128,256]{1,0:T(8,128)S(1)}, bf16[256,4096]{1,0:T(8,128)(2,1)S(1)}) custom-call(s32[1,64]{1,0:T(1,128)S(1)} %copy-done.7, s32[1]{0:T(128)S(6)} %copy.14.count_ref, f32[1024,1024]{1,0:T(8,128)S(1)} %copy-done.2, f32[1024,256]{1,0:T(8,128)S(1)} %copy-done.5, bf16[1792,1024]{1,0:T(8,128)(2,1)S(1)} %copy-done.3, ...), custom_call_target="tpu_custom_call" | custom-call | flops 4000000000 | bytes 11000000 | tf_op jit(solution)/shard_map/pallas_call | solution.py:417
  41.0 1.3 %copy-done = bf16[256,4096]{1,0:T(8,128)(2,1)} copy-done((bf16[256,4096]{1,0:T(8,128)(2,1)}, bf16[256,4096]{1,0:T(8,128)(2,1)S(1)}, u32[]{:S(2)}) %copy-start) | copy-done | bytes 2097176
  42.3 12.4 %all-to-all-done.refs_0_ = bf16[128,32,256]{2,1,0:T(8,128)(2,1)S(1)} async-done(((bf16[128,32,256]{2,1,0:T(8,128)(2,1)}), bf16[128,32,256]{2,1,0:T(8,128)(2,1)S(1)}, u32[]{:S(2)}, u32[]{:S(2)}) %all-to-all-start) | async-done | bytes 2097184 | tf_op jit(solution)/shard_map/all_to_all | solution.py:479
  54.7 1.4 %copy-done.9 = f32[512,768]{1,0:T(8,128)S(1)} copy-done((f32[512,768]{1,0:T(8,128)S(1)}, f32[512,768]{1,0:T(8,128)}, u32[]{:S(2)}) %copy-start.9) | copy-done | bytes 1572888
  56.1 5.0 %shard_map.116 = (f32[512,256]{1,0:T(8,128)}, bf16[128,56,128]{2,1,0:T(8,128)(2,1)S(1)}) custom-call(bf16[128,32,256]{2,1,0:T(8,128)(2,1)S(1)} %all-to-all-done.refs_0_, f32[512,768]{1,0:T(8,128)S(1)} %copy-done.9), custom_call_target="tpu_custom_call" | custom-call | flops 3000000000 | bytes 5000000 | tf_op jit(solution)/shard_map/pallas_call | solution.py:417
  61.1 31.9 %all_to_all.15.refs_2_ = bf16[128,56,128]{2,1,0:T(8,128)(2,1)S(1)} all-to-all(bf16[128,56,128]{2,1,0:T(8,128)(2,1)S(1)} %get-tuple-element.19), channel_id=1, replica_groups=mesh['row'=16,'col'=8] {'row','col'}, dimensions={0} | all-to-all | bytes 3670016 | tf_op jit(solution)/shard_map/all_to_all | solution.py:479
  93.1 1.8 %shard_map.117 = (bf16[128,256]{1,0:T(8,128)(2,1)S(1)}, bf16[16,128,256]{2,1,0:T(8,128)(2,1)}) custom-call(f32[128,256]{1,0:T(8,128)S(1)} %get-tuple-element.18.refs_0_, bf16[256,4096]{1,0:T(8,128)(2,1)S(1)} %copy-done.1, bf16[128,56,128]{2,1,0:T(8,128)(2,1)S(1)} %all_to_all.15.refs_2_), custom_call_target="tpu_custom_call" | custom-call | flops 600000000 | bytes 5000000 | tf_op jit(solution)/shard_map/pallas_call | solution.py:417
  94.8 3.7 %all-to-all-start.2 = ((bf16[16,128,256]{2,1,0:T(8,128)(2,1)}), bf16[16,128,256]{2,1,0:T(8,128)(2,1)S(1)}, u32[]{:S(2)}, u32[]{:S(2)}) async-start(bf16[16,128,256]{2,1,0:T(8,128)(2,1)} %get-tuple-element.21), calls=%async_computation.2 | async-start | bytes 2097152 | tf_op jit(solution)/shard_map/all_to_all | solution.py:548
  98.5 0.1 collective-permute-start
  98.6 1.2 %collective-permute-done = bf16[128,256]{1,0:T(8,128)(2,1)S(1)} collective-permute-done((bf16[128,256]{1,0:T(8,128)(2,1)S(1)}, bf16[128,256]{1,0:T(8,128)(2,1)S(1)}, u32[]{:S(2)}, u32[]{:S(2)}) %collective-permute-start) | collective-permute-done | bytes 65568 | tf_op jit(solution)/shard_map/ppermute | solution.py:551
  99.8 0.6 collective-permute-start.3
  100.4 2.1 %collective-permute-start.2 = (bf16[2,128,256]{2,1,0:T(8,128)(2,1)S(1)}, bf16[2,128,256]{2,1,0:T(8,128)(2,1)S(1)}, u32[]{:S(2)}, u32[]{:S(2)}) collective-permute-start(bf16[2,128,256]{2,1,0:T(8,128)(2,1)S(1)} %pad_maximum_fusion.pair), channel_id=1, source_target_pairs={{0,4},{1,5},{2,6},{3,7},{4,0},{5,1},{6,2},{7,3},{8,12},{9,13},{10,... | collective-permute-start | bytes 393224 | tf_op jit(solution)/shard_map/ppermute | solution.py:554
  102.6 1.4 %collective-permute-start.1 = (bf16[2,128,256]{2,1,0:T(8,128)(2,1)S(1)}, bf16[2,128,256]{2,1,0:T(8,128)(2,1)S(1)}, u32[]{:S(2)}, u32[]{:S(2)}) collective-permute-start(bf16[2,128,256]{2,1,0:T(8,128)(2,1)S(1)} %pad_maximum_fusion.pair), channel_id=1, source_target_pairs={{0,2},{1,3},{2,0},{3,1},{4,6},{5,7},{6,4},{7,5},{8,10},{9,11},{10,... | collective-permute-start | bytes 393224 | tf_op jit(solution)/shard_map/ppermute | solution.py:554
  104.0 5.5 %collective-permute-done.3.refs_2_ = bf16[2,128,256]{2,1,0:T(8,128)(2,1)S(1)} collective-permute-done((bf16[2,128,256]{2,1,0:T(8,128)(2,1)S(1)}, bf16[2,128,256]{2,1,0:T(8,128)(2,1)S(1)}, u32[]{:S(2)}, u32[]{:S(2)}) %collective-permute-start.3) | collective-permute-done | bytes 131104 | tf_op jit(solution)/shard_map/ppermute | solution.py:554
  109.5 0.0 collective-permute-done.2.refs_1_
  109.5 0.6 collective-permute-done.1.refs_0_
  110.1 6.1 %all-to-all-done.2 = bf16[16,128,256]{2,1,0:T(8,128)(2,1)S(1)} async-done(((bf16[16,128,256]{2,1,0:T(8,128)(2,1)}), bf16[16,128,256]{2,1,0:T(8,128)(2,1)S(1)}, u32[]{:S(2)}, u32[]{:S(2)}) %all-to-all-start.2) | async-done | bytes 1048608 | tf_op jit(solution)/shard_map/all_to_all | solution.py:548
  116.2 3.8 %shard_map.118 = f32[1024,2048]{1,0:T(8,128)} custom-call(s32[1]{0:T(128)} %bitcast.me_ref, bf16[2,128,256]{2,1,0:T(8,128)(2,1)S(1)} %pad_maximum_fusion.pair, bf16[2,128,256]{2,1,0:T(8,128)(2,1)S(1)} %collective-permute-done.1.refs_0_, bf16[2,128,256]{2,1,0:T(8,128)(2,1)S(1)} %collective-permute-done.2.refs_1_, ...), custom_call_target="tpu_custom_call" | custom-call | flops 1000000000 | bytes 10000000 | tf_op jit(solution)/shard_map/pallas_call | solution.py:417
  (18 shorter events, 0.0 us)
Async XLA Ops:
  13.2 11.4 %copy-start.12 = (f32[128,8]{0,1:T(8,128)S(1)}, f32[128,8]{0,1:T(8,128)}, u32[]{:S(2)}) copy-start(f32[128,8]{0,1:T(8,128)} %param.18) | copy-start | bytes 12292
  13.2 11.5 %copy-start.13 = (s32[128,8]{0,1:T(8,128)S(1)}, s32[128,8]{0,1:T(8,128)}, u32[]{:S(2)}) copy-start(s32[128,8]{0,1:T(8,128)} %param.19) | copy-start | bytes 12292
  13.2 11.6 %copy-start.4 = (f32[512,512]{1,0:T(8,128)S(1)}, f32[512,512]{1,0:T(8,128)}, u32[]{:S(2)}) copy-start(f32[512,512]{1,0:T(8,128)} %sep_hbm.1) | copy-start | bytes 3145732
  13.2 41.5 %all-to-all-start = ((bf16[128,32,256]{2,1,0:T(8,128)(2,1)}), bf16[128,32,256]{2,1,0:T(8,128)(2,1)S(1)}, u32[]{:S(2)}, u32[]{:S(2)}) async-start(bf16[128,32,256]{2,1,0:T(8,128)(2,1)} %get-tuple-element.12), calls=%async_computation | async-start | bytes 4194304 | tf_op jit(solution)/shard_map/all_to_all | solution.py:479
  24.8 1.0 copy-start.6
  25.8 5.5 %copy-start.2 = (f32[1024,1024]{1,0:T(8,128)S(1)}, f32[1024,1024]{1,0:T(8,128)}, u32[]{:S(2)}) copy-start(f32[1024,1024]{1,0:T(8,128)} %factor.3) | copy-start | bytes 12582916
  25.8 5.5 %copy-start.5 = (f32[1024,256]{1,0:T(8,128)S(1)}, f32[1024,256]{1,0:T(8,128)}, u32[]{:S(2)}) copy-start(f32[1024,256]{1,0:T(8,128)} %rhs.3) | copy-start | bytes 3145732
  25.8 5.5 %copy-start.7 = (s32[1,64]{1,0:T(1,128)S(1)}, s32[1,64]{1,0:T(1,128)}, u32[]{:S(2)}) copy-start(s32[1,64]{1,0:T(1,128)} %owner_ref.3) | copy-start | bytes 772
  25.8 5.5 %copy-start.10 = (bf16[2,512,512]{2,1,0:T(8,128)(2,1)S(1)}, bf16[2,512,512]{2,1,0:T(8,128)(2,1)}, u32[]{:S(2)}) copy-start(bf16[2,512,512]{2,1,0:T(8,128)(2,1)} %get-tuple-element.13.high_hbm) | copy-start | bytes 3145732
  25.8 5.5 %copy-start.11 = (bf16[2,512,512]{2,1,0:T(8,128)(2,1)S(1)}, bf16[2,512,512]{2,1,0:T(8,128)(2,1)}, u32[]{:S(2)}) copy-start(bf16[2,512,512]{2,1,0:T(8,128)(2,1)} %get-tuple-element.14.low_hbm) | copy-start | bytes 3145732
  30.2 1.1 copy-start.8
  31.4 2.0 %copy-start.3 = (bf16[1792,1024]{1,0:T(8,128)(2,1)S(1)}, bf16[1792,1024]{1,0:T(8,128)(2,1)}, u32[]{:S(2)}) copy-start(bf16[1792,1024]{1,0:T(8,128)(2,1)} %coupling.3) | copy-start | bytes 11010052
  41.0 1.3 %copy-start = (bf16[256,4096]{1,0:T(8,128)(2,1)}, bf16[256,4096]{1,0:T(8,128)(2,1)S(1)}, u32[]{:S(2)}) copy-start(bf16[256,4096]{1,0:T(8,128)(2,1)S(1)} %get-tuple-element.15.refs_1_) | copy-start | bytes 6291460
  54.7 1.4 %copy-start.9 = (f32[512,768]{1,0:T(8,128)S(1)}, f32[512,768]{1,0:T(8,128)}, u32[]{:S(2)}) copy-start(f32[512,768]{1,0:T(8,128)} %copy-done.8) | copy-start | bytes 4718596
  61.1 31.9 %copy-start.1 = (bf16[256,4096]{1,0:T(8,128)(2,1)S(1)}, bf16[256,4096]{1,0:T(8,128)(2,1)}, u32[]{:S(2)}) copy-start(bf16[256,4096]{1,0:T(8,128)(2,1)} %copy-done) | copy-start | bytes 6291460
  94.8 21.4 %all-to-all-start.2 = ((bf16[16,128,256]{2,1,0:T(8,128)(2,1)}), bf16[16,128,256]{2,1,0:T(8,128)(2,1)S(1)}, u32[]{:S(2)}, u32[]{:S(2)}) async-start(bf16[16,128,256]{2,1,0:T(8,128)(2,1)} %get-tuple-element.21), calls=%async_computation.2 | async-start | bytes 2097152 | tf_op jit(solution)/shard_map/all_to_all | solution.py:548
  98.5 1.3 %collective-permute-start = (bf16[128,256]{1,0:T(8,128)(2,1)S(1)}, bf16[128,256]{1,0:T(8,128)(2,1)S(1)}, u32[]{:S(2)}, u32[]{:S(2)}) collective-permute-start(bf16[128,256]{1,0:T(8,128)(2,1)S(1)} %get-tuple-element.20), channel_id=1, source_target_pairs={{0,1},{1,0},{2,3},{3,2},{4,5},{5,4},{6,7},{7,6},{8,9},{9,8},{10,11... | collective-permute-start | bytes 196616 | tf_op jit(solution)/shard_map/ppermute | solution.py:551
  99.8 9.7 %collective-permute-start.3 = (bf16[2,128,256]{2,1,0:T(8,128)(2,1)S(1)}, bf16[2,128,256]{2,1,0:T(8,128)(2,1)S(1)}, u32[]{:S(2)}, u32[]{:S(2)}) collective-permute-start(bf16[2,128,256]{2,1,0:T(8,128)(2,1)S(1)} %pad_maximum_fusion.pair), channel_id=1, source_target_pairs={{0,6},{1,7},{2,4},{3,5},{4,2},{5,3},{6,0},{7,1},{8,14},{9,15},{10,... | collective-permute-start | bytes 393224 | tf_op jit(solution)/shard_map/ppermute | solution.py:554
  100.4 9.1 %collective-permute-start.2 = (bf16[2,128,256]{2,1,0:T(8,128)(2,1)S(1)}, bf16[2,128,256]{2,1,0:T(8,128)(2,1)S(1)}, u32[]{:S(2)}, u32[]{:S(2)}) collective-permute-start(bf16[2,128,256]{2,1,0:T(8,128)(2,1)S(1)} %pad_maximum_fusion.pair), channel_id=1, source_target_pairs={{0,4},{1,5},{2,6},{3,7},{4,0},{5,1},{6,2},{7,3},{8,12},{9,13},{10,... | collective-permute-start | bytes 393224 | tf_op jit(solution)/shard_map/ppermute | solution.py:554
  102.6 7.5 %collective-permute-start.1 = (bf16[2,128,256]{2,1,0:T(8,128)(2,1)S(1)}, bf16[2,128,256]{2,1,0:T(8,128)(2,1)S(1)}, u32[]{:S(2)}, u32[]{:S(2)}) collective-permute-start(bf16[2,128,256]{2,1,0:T(8,128)(2,1)S(1)} %pad_maximum_fusion.pair), channel_id=1, source_target_pairs={{0,2},{1,3},{2,0},{3,1},{4,6},{5,7},{6,4},{7,5},{8,10},{9,11},{10,... | collective-permute-start | bytes 393224 | tf_op jit(solution)/shard_map/ppermute | solution.py:554
